TPU v7x, 512 devices: a whole 4x8x8 slice. The times are simulated.
512 devices in a mesh: gx: 32 (over z, x), gy: 16 (over y, core).
Axes of the slice: x: 4, y: 8, z: 8, core: 2. Of those that a mesh axis runs over, the one named last changes fastest.
Arguments:
- probe_data: float32 [2, 3, 65536], P(None, None, ('gx', 'gy')), may hold values from -10 to 10
- conductivity: float32 [160, 80, 640], P('gx', 'gy'), may hold values from 0.5 to 10
- support: int32 [32, 16, 128], P('gx', 'gy'), may hold values 0 or 1
- face_tags: int32 [2, 32, 16], P(None, 'gx', 'gy'), may hold values 0 or 1
- probe_nodes: int32 [65536], P(('gx', 'gy')), may hold values from 0 to 15999
Outputs:
- source_estimate: float32 [2, 3, 160, 80, 640], P(None, None, 'gx', 'gy')
- data_residual: float32 [2, 3, 65536], P(None, None, ('gx', 'gy'))
Inputs may be any that keep to these rules, and one draw needn't show every extreme that they name: `probe_nodes`: probe p lies in the block of device p // 128 (gx-major), as a node index of that block flattened with the third dimension fastest.
All inputs are finite; a program needn't handle non-finite values. No bound on the sum of `support` or of `face_tags` on one device may be relied on, other than what follows from the above.
Results may differ from a plain program's by a relative error of at most 0.0008.
Values sent between devices are 32-bit elements; how exact they have to be, the bound alone decides.
A program may use at most 128 MiB of HBM per device.

v0:
```python
import math

import jax
import jax.numpy as jnp
import numpy as np
from jax import lax
from jax.sharding import PartitionSpec as P

ITERS = 2


STEP_SIZE = 0.02
LIFT_HALF = 5.0
DRIVE_GAIN = 50.0


def with_halo(x, sides, width):
    for axis, dim in sides:
        size, length = (lax.axis_size(axis), x.shape[dim])
        up = [(i, (i + 1) % size) for i in range(size - 1)]
        down = [(j, i) for i, j in up]
        last = lax.slice_in_dim(x, length - width, length, axis=dim)
        leading = lax.slice_in_dim(x, 0, width, axis=dim)
        before = lax.ppermute(last, axis, up)
        after = lax.ppermute(leading, axis, down)
        x = jnp.concatenate([before, x, after], axis=dim)
    return x


def lobatto_table():
    radical = math.sqrt(3.0 / 7.0)
    points = np.array([-1.0, -radical, 0.0, radical, 1.0])
    legendre = (35.0 * points**4 - 30.0 * points**2 + 3.0) / 8.0
    matrix = np.zeros((5, 5))
    for row_idx in range(5):
        for col_idx in range(5):
            if row_idx != col_idx:
                matrix[row_idx, col_idx] = legendre[row_idx] / (
                    legendre[col_idx] * (points[row_idx] - points[col_idx])
                )
    matrix[0, 0] = -5.0
    matrix[4, 4] = 5.0
    return np.asarray(matrix, dtype=np.float32)


def apply_lobatto(blocks, node_axis, lobatto):
    results = []
    for row_idx in range(5):
        total = None
        for col_idx in range(5):
            weight = float(lobatto[row_idx, col_idx])
            if weight == 0.0:
                continue
            term = weight * lax.index_in_dim(blocks, col_idx, node_axis, keepdims=False)
            total = term if total is None else total + term
        results.append(total)
    return jnp.stack(results, axis=node_axis)


def normal_cross(axis_id, orient, vector):
    blank_part = jnp.zeros_like(vector[0])
    if axis_id == 0:
        return [blank_part, -orient * vector[2], orient * vector[1]]
    if axis_id == 1:
        return [orient * vector[2], blank_part, -orient * vector[0]]
    return [-orient * vector[1], orient * vector[0], blank_part]


def face_flux(inner, outer, axis_id, orient):
    jumps = outer - inner
    jump_e = [jumps[0], jumps[1], jumps[2]]
    jump_h = [jumps[3], jumps[4], jumps[5]]
    turn_h = normal_cross(axis_id, orient, jump_h)
    turn_e = normal_cross(axis_id, orient, jump_e)
    pieces = []
    for member in range(3):
        retain = 0.0 if member == axis_id else 1.0
        pieces.append(turn_h[member] + retain * jump_e[member])
    for member in range(3):
        retain = 0.0 if member == axis_id else 1.0
        pieces.append(retain * jump_h[member] - turn_e[member])
    return LIFT_HALF * jnp.stack(pieces)


def add_faces(change, fields, ghost_low, ghost_high, axis_dim):
    extent = fields.shape
    blocks = fields.reshape(extent[:axis_dim] + (extent[axis_dim] // 5, 5) + extent[axis_dim + 1 :])
    low_faces = lax.index_in_dim(blocks, 0, axis_dim + 1, keepdims=False)
    high_faces = lax.index_in_dim(blocks, 4, axis_dim + 1, keepdims=False)
    elements = low_faces.shape[axis_dim]
    outer_low = jnp.concatenate(
        [
            jnp.expand_dims(ghost_low, axis_dim),
            lax.slice_in_dim(high_faces, 0, elements - 1, axis=axis_dim),
        ],
        axis=axis_dim,
    )
    outer_high = jnp.concatenate(
        [
            lax.slice_in_dim(low_faces, 1, elements, axis=axis_dim),
            jnp.expand_dims(ghost_high, axis_dim),
        ],
        axis=axis_dim,
    )
    fix_low = face_flux(low_faces, outer_low, axis_dim - 1, -1.0)
    fix_high = face_flux(high_faces, outer_high, axis_dim - 1, 1.0)
    middle_zero = jnp.zeros_like(fix_low)
    stacked = jnp.stack(
        [fix_low, middle_zero, middle_zero, middle_zero, fix_high], axis=axis_dim + 1
    )
    return change + stacked.reshape(extent)


def add_depth_faces(change, fields, tag_nodes):
    extent = fields.shape
    blocks = fields.reshape(extent[:3] + (5, extent[3] // 5))
    low_faces = blocks[:, :, :, 0]
    high_faces = blocks[:, :, :, 4]
    mirror = jnp.array([-1.0, -1.0, -1.0, 1.0, 1.0, 1.0], dtype=jnp.float32)[:, None, None]
    bottom = mirror * tag_nodes[0] * low_faces[:, :, :, 0]
    top_ghost = mirror * tag_nodes[1] * high_faces[:, :, :, -1]
    outer_low = jnp.concatenate([bottom[..., None], high_faces[..., :-1]], axis=3)
    outer_high = jnp.concatenate([low_faces[..., 1:], top_ghost[..., None]], axis=3)
    fix_low = face_flux(low_faces, outer_low, 2, -1.0)
    fix_high = face_flux(high_faces, outer_high, 2, 1.0)
    middle_zero = jnp.zeros_like(fix_low)
    stacked = jnp.stack([fix_low, middle_zero, middle_zero, middle_zero, fix_high], axis=3)
    return change + stacked.reshape(extent)


def derivative_first(fields, lobatto):
    extent = fields.shape
    blocks = fields.reshape(extent[0], extent[1] // 5, 5, extent[2], extent[3])
    return apply_lobatto(blocks, 2, lobatto).reshape(extent)


def derivative_second(fields, lobatto):
    extent = fields.shape
    blocks = fields.reshape(extent[0], extent[1], extent[2] // 5, 5, extent[3])
    return apply_lobatto(blocks, 3, lobatto).reshape(extent)


def derivative_depth(fields, lobatto):
    extent = fields.shape
    blocks = fields.reshape(extent[0], extent[1], extent[2], 5, extent[3] // 5)
    return apply_lobatto(blocks, 3, lobatto).reshape(extent)


def evaluate(fields, ghosts, conduct, tag_nodes, lobatto):
    grad_x = derivative_first(fields, lobatto)
    grad_y = derivative_second(fields, lobatto)
    grad_z = derivative_depth(fields, lobatto)
    curl_e = [grad_y[2] - grad_z[1], grad_z[0] - grad_x[2], grad_x[1] - grad_y[0]]
    curl_h = [grad_y[5] - grad_z[4], grad_z[3] - grad_x[5], grad_x[4] - grad_y[3]]
    change = jnp.stack(
        [
            curl_h[0] - conduct * fields[0],
            curl_h[1] - conduct * fields[1],
            curl_h[2] - conduct * fields[2],
            -curl_e[0],
            -curl_e[1],
            -curl_e[2],
        ]
    )
    change = add_faces(change, fields, ghosts[0], ghosts[1], 1)
    change = add_faces(change, fields, ghosts[2], ghosts[3], 2)
    return add_depth_faces(change, fields, tag_nodes)


def element_inner(array):
    extent = array.shape
    return jnp.swapaxes(array.reshape(extent[:-1] + (extent[-1] // 5, 5)), -1, -2).reshape(extent)


def element_outer(array):
    extent = array.shape
    return jnp.swapaxes(array.reshape(extent[:-1] + (5, extent[-1] // 5)), -1, -2).reshape(extent)


def data_norm(vector):
    return jnp.sqrt(lax.psum(jnp.sum(vector * vector), ("gx", "gy")))


def source_norm(vector):
    return jnp.sqrt(lax.psum(jnp.sum(vector * vector), ("gx", "gy")))


def shards(probe_data, conductivity, support, face_tags, probe_nodes):
    lobatto = lobatto_table()
    depth_nodes = conductivity.shape[2]
    depth_elems = depth_nodes // 5
    conduct_inner = element_inner(conductivity)
    support_nodes = jnp.tile(
        jnp.repeat(jnp.repeat(support, 5, axis=0), 5, axis=1), (1, 1, 5)
    ).astype(jnp.float32)
    tag_nodes = jnp.repeat(jnp.repeat(face_tags, 5, axis=1), 5, axis=2).astype(jnp.float32)
    rows_x = conductivity.shape[0]
    rows_y = conductivity.shape[1]
    node_count = rows_x * rows_y * depth_nodes
    depth_pos = probe_nodes % depth_nodes
    probe_inner = (probe_nodes - depth_pos + depth_pos % 5 * depth_elems + depth_pos // 5).astype(
        jnp.int32
    )

    def local_rates(fields, ghosts):
        return evaluate(fields, ghosts, conduct_inner, tag_nodes, lobatto)

    def widen_faces(fields):
        padded = with_halo(fields, (("gx", 1), ("gy", 2)), 1)
        return (padded[:, 0, 1:-1], padded[:, -1, 1:-1], padded[:, 1:-1, 0], padded[:, 1:-1, -1])

    def apply_rates(fields):
        return local_rates(fields, widen_faces(fields))

    blank_field = jnp.zeros((6, rows_x, rows_y, depth_nodes), jnp.float32)
    plane_x = jnp.zeros((6, rows_y, depth_nodes), jnp.float32)
    plane_y = jnp.zeros((6, rows_x, depth_nodes), jnp.float32)
    pullback = jax.vjp(local_rates, blank_field, (plane_x, plane_x, plane_y, plane_y))[1]

    def transpose_rates(cotangent):
        own_part, ghost_cots = pullback(cotangent)
        padded = jnp.pad(own_part, ((0, 0), (1, 1), (1, 1), (0, 0)))
        padded = padded.at[:, 0, 1:-1].set(ghost_cots[0]).at[:, -1, 1:-1].set(ghost_cots[1])
        padded = padded.at[:, 1:-1, 0].set(ghost_cots[2]).at[:, 1:-1, -1].set(ghost_cots[3])
        got_all = with_halo(padded, (("gx", 1), ("gy", 2)), 1)
        low_x = got_all[:, 0, 2 : rows_y + 2]
        high_x = got_all[:, -1, 2 : rows_y + 2]
        low_y = got_all[:, 2 : rows_x + 2, 0]
        high_y = got_all[:, 2 : rows_x + 2, -1]
        return (
            own_part.at[:, 0]
            .add(low_x)
            .at[:, -1]
            .add(high_x)
            .at[:, :, 0]
            .add(low_y)
            .at[:, :, -1]
            .add(high_y)
        )

    def adjoint(values):
        steps_all = values.shape[0]
        carried = blank_field
        outputs = [None] * steps_all
        for moment in reversed(range(steps_all)):
            injected = (
                jnp.zeros((3, node_count), jnp.float32).at[:, probe_inner].add(values[moment])
            )
            carried = carried.at[0:3].add(injected.reshape(3, rows_x, rows_y, depth_nodes))
            first_pass = transpose_rates(carried)
            outputs[moment] = (
                -DRIVE_GAIN
                * support_nodes
                * (STEP_SIZE * carried[0:3] + 0.5 * STEP_SIZE * STEP_SIZE * first_pass[0:3])
            )
            if moment > 0:
                second_pass = transpose_rates(first_pass)
                carried = (
                    carried + STEP_SIZE * first_pass + 0.5 * STEP_SIZE * STEP_SIZE * second_pass
                )
        return jnp.stack(outputs)

    def apart_step(raw_left, right_vector, final_sweep):
        data_scale = data_norm(raw_left)
        left_vector = raw_left / data_scale
        if final_sweep:
            return (data_scale, left_vector, data_scale, right_vector)
        raw_right = adjoint(left_vector) - data_scale * right_vector
        source_scale = source_norm(raw_right)
        return (data_scale, left_vector, source_scale, raw_right / source_scale)

    data_scale = data_norm(probe_data)
    left_vector = probe_data / data_scale
    raw_right = adjoint(left_vector)
    source_scale = source_norm(raw_right)
    right_vector = raw_right / source_scale
    direction = right_vector
    estimate = jnp.zeros_like(right_vector)
    phi_bar = data_scale
    rho_bar = source_scale
    for sweep in range(ITERS):
        final_sweep = sweep == ITERS - 1
        forward_fields = blank_field
        blank_three = jnp.zeros((3, rows_x, rows_y, depth_nodes), jnp.float32)
        records = []
        for forward_moment in range(right_vector.shape[0]):
            forcing = jnp.concatenate(
                [-DRIVE_GAIN * support_nodes * right_vector[forward_moment], blank_three]
            )
            slope_one = forcing if forward_moment == 0 else apply_rates(forward_fields) + forcing
            middle = forward_fields + STEP_SIZE * slope_one
            slope_two = apply_rates(middle) + forcing
            forward_fields = forward_fields + 0.5 * STEP_SIZE * (slope_one + slope_two)
            records.append(
                jnp.take(forward_fields[0:3].reshape(3, node_count), probe_inner, axis=1)
            )
        raw_left = jnp.stack(records) - source_scale * left_vector
        data_scale, left_vector, next_scale, next_right = apart_step(
            raw_left, right_vector, final_sweep
        )
        rho_value = jnp.sqrt(rho_bar * rho_bar + data_scale * data_scale)
        cosine = rho_bar / rho_value
        sine_value = data_scale / rho_value
        phi_step = cosine * phi_bar
        phi_bar = sine_value * phi_bar
        estimate = estimate + phi_step / rho_value * direction
        if not final_sweep:
            source_scale = next_scale
            right_vector = next_right
            theta_next = sine_value * source_scale
            rho_bar = -cosine * source_scale
            direction = right_vector - theta_next / rho_value * direction
    return (element_outer(estimate), phi_bar * left_vector)


def solution(mesh):
    return jax.shard_map(
        shards,
        mesh=mesh,
        in_specs=(
            P(None, None, ("gx", "gy")),
            P("gx", "gy", None),
            P("gx", "gy", None),
            P(None, "gx", "gy"),
            P(("gx", "gy")),
        ),
        out_specs=(P(None, None, "gx", "gy", None), P(None, None, ("gx", "gy"))),
        check_vma=False,
    )
```

profile of v0, /device:TPU:1, one launch (start us, length us, event | category | flops | bytes accessed | tf_op | source)
XLA Modules:
  0.0 1055.4 jit_solution(4896771559007851966)
XLA Ops:
  1.9 106.1 %psum.35 = f32[]{:T(128)} all-reduce(f32[]{:T(128)} %multiply_reduce_fusion.4), channel_id=1, replica_groups=mesh['gx'=32,'gy'=16] {'gx','gy'}, use_global_device_ids=true, to_apply=%region_1.2 | all-reduce | flops 1 | bytes 8 | tf_op jit(solution)/shard_map/psum | solution.py:181
  115.6 17.3 %slice_reduce_fusion.5 = (f32[16000]{0:T(1024)S(1)}, f32[16000]{0:T(1024)S(1)}, f32[16000]{0:T(1024)S(1)}) fusion(f32[3,16000]{0,1:T(8,128)} %scatter_custom_fusion), kind=kLoop, calls=%fused_computation.13 | loop fusion | bytes 384000 | tf_op jit(solution)/shard_map/transpose(jvp())/unstack | solution.py:155
  138.4 6.1 copy.11689
  175.9 6.7 copy.11727
  187.5 6.7 copy.11764
  220.6 5.4 collective-permute-start.6
  248.2 5.2 collective-permute-start.10
  257.1 106.6 %psum.36 = f32[]{:T(128)} all-reduce(f32[]{:T(128)} %multiply_reduce_fusion.1), channel_id=1, replica_groups=mesh['gx'=32,'gy'=16] {'gx','gy'}, use_global_device_ids=true, to_apply=%region_5.6 | all-reduce | flops 1 | bytes 8 | tf_op jit(solution)/shard_map/psum | solution.py:185
  387.6 4.9 collective-permute-start.14
  456.7 5.5 copy.11866
  462.2 5.5 copy.11988
  476.7 107.2 %psum.37 = f32[]{:T(128)} all-reduce(f32[]{:T(128)} %get-tuple-element.671), channel_id=1, replica_groups=mesh['gx'=32,'gy'=16] {'gx','gy'}, use_global_device_ids=true, to_apply=%region_7.9 | all-reduce | flops 1 | bytes 8 | tf_op jit(solution)/shard_map/psum | solution.py:181
  590.3 17.3 %slice_reduce_fusion.2 = (f32[16000]{0:T(1024)S(1)}, f32[16000]{0:T(1024)S(1)}, f32[16000]{0:T(1024)S(1)}) fusion(f32[3,16000]{0,1:T(8,128)} %scatter_custom_fusion.2), kind=kLoop, calls=%fused_computation.10 | loop fusion | bytes 384000 | tf_op jit(solution)/shard_map/transpose(jvp())/unstack | solution.py:155
  613.2 6.2 copy.11993
  631.6 6.2 copy.12023
  637.9 5.3 scatter_custom_fusion.3
  643.2 6.7 copy.12081
  709.5 5.5 collective-permute-start.34
  718.8 110.4 %psum.38 = f32[]{:T(128)} all-reduce(f32[]{:T(128)} %multiply_reduce_fusion), channel_id=1, replica_groups=mesh['gx'=32,'gy'=16] {'gx','gy'}, use_global_device_ids=true, to_apply=%region_11.13 | all-reduce | flops 1 | bytes 8 | tf_op jit(solution)/shard_map/psum | solution.py:185
  910.8 5.5 copy.12187
  920.4 5.5 copy.12286
  930.9 107.9 %psum.39 = f32[]{:T(128)} all-reduce(f32[]{:T(128)} %get-tuple-element.661), channel_id=1, replica_groups=mesh['gx'=32,'gy'=16] {'gx','gy'}, use_global_device_ids=true, to_apply=%region_13.15 | all-reduce | flops 1 | bytes 8 | tf_op jit(solution)/shard_map/psum | solution.py:181
  1039.9 5.9 copy.12289
  1045.8 8.6 reshape.10785
  (1018 shorter events, 370.1 us)
Async XLA Ops:
  170.4 24.5 %collective-permute-start.1 = (f32[6,1,7,640]{3,0,2,1:T(8,128)S(1)}, f32[6,1,7,640]{3,0,2,1:T(8,128)S(1)}, u32[]{:S(2)}, u32[]{:S(2)}) collective-permute-start(f32[6,1,7,640]{3,0,2,1:T(8,128)S(1)} %get-tuple-element.715), channel_id=1, source_target_pairs={{16,0},{32,16},{48,32},{64,48},{80,64},{96,80},{112,96},{128,112},... | collective-permute-start | bytes 322568 | tf_op jit(solution)/shard_map/ppermute | solution.py:25
  171.7 23.2 %collective-permute-start = (f32[6,1,7,640]{3,0,2,1:T(8,128)S(1)}, f32[6,1,7,640]{3,0,2,1:T(8,128)S(1)}, u32[]{:S(2)}, u32[]{:S(2)}) collective-permute-start(f32[6,1,7,640]{3,0,2,1:T(8,128)S(1)} %get-tuple-element.716), channel_id=1, source_target_pairs={{0,16},{16,32},{32,48},{48,64},{64,80},{80,96},{96,112},{112,128},... | collective-permute-start | bytes 322568 | tf_op jit(solution)/shard_map/ppermute | solution.py:24
  194.9 8.4 collective-permute-start.3
  210.2 8.4 collective-permute-start.5
  218.7 9.4 collective-permute-start.7
  246.3 9.7 collective-permute-start.11
  367.0 18.5 %collective-permute-start.12 = (f32[6,1,5,640]{3,0,2,1:T(8,128)}, f32[6,1,5,640]{3,0,2,1:T(8,128)}, u32[]{:S(2)}, u32[]{:S(2)}) collective-permute-start(f32[6,1,5,640]{3,0,2,1:T(8,128)} %get-tuple-element.1107), channel_id=1, source_target_pairs={{0,16},{16,32},{32,48},{48,64},{64,80},{80,96},{96,112},{112,128},... | collective-permute-start | bytes 230408 | tf_op jit(solution)/shard_map/ppermute | solution.py:24
  371.3 14.2 %collective-permute-start.13 = (f32[6,1,5,640]{3,0,2,1:T(8,128)}, f32[6,1,5,640]{3,0,2,1:T(8,128)}, u32[]{:S(2)}, u32[]{:S(2)}) collective-permute-start(f32[6,1,5,640]{3,0,2,1:T(8,128)} %get-tuple-element.1108), channel_id=1, source_target_pairs={{16,0},{32,16},{48,32},{64,48},{80,64},{96,80},{112,96},{128,112},... | collective-permute-start | bytes 230408 | tf_op jit(solution)/shard_map/ppermute | solution.py:25
  402.2 13.1 %collective-permute-start.16 = (f32[6,1,5,640]{3,0,2,1:T(8,128)S(1)}, f32[6,1,5,640]{3,0,2,1:T(8,128)S(1)}, u32[]{:S(2)}, u32[]{:S(2)}) collective-permute-start(f32[6,1,5,640]{3,0,2,1:T(8,128)S(1)} %get-tuple-element.1095), channel_id=1, source_target_pairs={{0,16},{16,32},{32,48},{48,64},{64,80},{80,96},{96,112},{112,128},... | collective-permute-start | bytes 230408 | tf_op jit(solution)/shard_map/ppermute | solution.py:24
  406.5 8.8 collective-permute-start.17
  427.9 14.7 %collective-permute-start.20 = (f32[6,1,5,640]{3,0,2,1:T(8,128)}, f32[6,1,5,640]{3,0,2,1:T(8,128)S(1)}, u32[]{:S(2)}, u32[]{:S(2)}) collective-permute-start(f32[6,1,5,640]{3,0,2,1:T(8,128)} %get-tuple-element.1074), channel_id=1, source_target_pairs={{0,16},{16,32},{32,48},{48,64},{64,80},{80,96},{96,112},{112,128},... | collective-permute-start | bytes 230408 | tf_op jit(solution)/shard_map/ppermute | solution.py:24
  432.2 10.4 collective-permute-start.21
  625.9 23.9 %collective-permute-start.25 = (f32[6,1,7,640]{3,0,1,2:T(8,128)S(1)}, f32[6,1,7,640]{3,0,1,2:T(8,128)S(1)}, u32[]{:S(2)}, u32[]{:S(2)}) collective-permute-start(f32[6,1,7,640]{3,0,1,2:T(8,128)S(1)} %get-tuple-element.709), channel_id=1, source_target_pairs={{16,0},{32,16},{48,32},{64,48},{80,64},{96,80},{112,96},{128,112},... | collective-permute-start | bytes 322568 | tf_op jit(solution)/shard_map/ppermute | solution.py:25
  627.2 22.6 %collective-permute-start.24 = (f32[6,1,7,640]{3,0,1,2:T(8,128)S(1)}, f32[6,1,7,640]{3,0,1,2:T(8,128)S(1)}, u32[]{:S(2)}, u32[]{:S(2)}) collective-permute-start(f32[6,1,7,640]{3,0,1,2:T(8,128)S(1)} %get-tuple-element.710), channel_id=1, source_target_pairs={{0,16},{16,32},{32,48},{48,64},{64,80},{80,96},{96,112},{112,128},... | collective-permute-start | bytes 322568 | tf_op jit(solution)/shard_map/ppermute | solution.py:24
  649.9 9.1 collective-permute-start.27
  666.0 11.0 %collective-permute-start.29 = (f32[6,1,7,640]{3,0,1,2:T(8,128)}, f32[6,1,7,640]{3,0,1,2:T(8,128)}, u32[]{:S(2)}, u32[]{:S(2)}) collective-permute-start(f32[6,1,7,640]{3,0,1,2:T(8,128)} %get-tuple-element.707), channel_id=1, source_target_pairs={{16,0},{32,16},{48,32},{64,48},{80,64},{96,80},{112,96},{128,112},... | collective-permute-start | bytes 322568 | tf_op jit(solution)/shard_map/ppermute | solution.py:25
  667.2 9.7 collective-permute-start.28
  677.9 9.1 collective-permute-start.31
  707.6 9.9 collective-permute-start.35
  832.4 18.7 %collective-permute-start.36 = (f32[6,1,5,640]{3,0,2,1:T(8,128)}, f32[6,1,5,640]{3,0,2,1:T(8,128)S(1)}, u32[]{:S(2)}, u32[]{:S(2)}) collective-permute-start(f32[6,1,5,640]{3,0,2,1:T(8,128)} %get-tuple-element.799), channel_id=1, source_target_pairs={{0,16},{16,32},{32,48},{48,64},{64,80},{80,96},{96,112},{112,128},... | collective-permute-start | bytes 230408 | tf_op jit(solution)/shard_map/ppermute | solution.py:24
  836.1 15.0 %collective-permute-start.37 = (f32[6,1,5,640]{3,0,2,1:T(8,128)}, f32[6,1,5,640]{3,0,2,1:T(8,128)}, u32[]{:S(2)}, u32[]{:S(2)}) collective-permute-start(f32[6,1,5,640]{3,0,2,1:T(8,128)} %get-tuple-element.800), channel_id=1, source_target_pairs={{16,0},{32,16},{48,32},{64,48},{80,64},{96,80},{112,96},{128,112},... | collective-permute-start | bytes 230408 | tf_op jit(solution)/shard_map/ppermute | solution.py:25
  866.5 10.2 collective-permute-start.41
  867.8 9.1 collective-permute-start.40
  888.6 8.1 collective-permute-start.44
  (128 other events, 2168.6 us)
where the time goes:
time: 1070 us; the launch traced here: 1060 us
  blocking collectives  538 us (50%)
  local copies, waits for them, and re-layouts  181 us (17%)
  other arithmetic  146 us (14%)
  starting transfers between devices  141 us (13%)
  waiting for transfers between devices  39 us (4%)
  between operations  11.2 us (1%)
    psum x3, blocking collectives, data_norm(): return jnp.sqrt(lax.psum(jnp.sum(vector * vector), ('gx', 'gy')))  321 us
    psum x2, blocking collectives, source_norm(): return jnp.sqrt(lax.psum(jnp.sum(vector * vector), ('gx', 'gy')))  217 us
    ppermute x24, starting transfers between devices, with_halo(): before = lax.ppermute(last, axis, up)  98.7 us
    another operation x15, local copies, waits for them, and re-layouts, evaluate(): jnp.stack([curl_h[0] - conduct * fields[0], curl_h[1] - conduct * fields[...  44.2 us
    ppermute x24, starting transfers between devices, with_halo(): after = lax.ppermute(leading, axis, down)  42.1 us
    add x5, local copies, waits for them, and re-layouts, adjoint(): carried.at[0:3].add(injected.reshape(3, rows_x, rows_y, depth_nodes))  25.2 us
    ppermute x24, waiting for transfers between devices, with_halo(): after = lax.ppermute(leading, axis, down)  24.8 us
    slice x4, local copies, waits for them, and re-layouts, shards(): forward_fields[0:3].reshape(3, node_count)  22.1 us
  transfers between devices with their start and end apart: 48, of which 16 were waited for; matrix products, arithmetic and copies ran while one was open for 10% of the time, Pallas kernels for 0%

commit v1 on v0

v1 whole, which is shorter than its diff:
```python
import functools
import math

import jax
import jax.numpy as jnp
import numpy as np
from jax import lax
from jax.experimental import pallas as pl
from jax.experimental.pallas import tpu as pltpu
from jax.sharding import PartitionSpec as P

MESH = pl.DeviceIdType.MESH
F32 = jnp.float32
BF16 = jnp.bfloat16

STEP_SIZE = 0.02
LIFT_HALF = 5.0
DRIVE_GAIN = 50.0
NX_CHIPS = 4
CORES = 2
ROWS = 80
QROWS = 56
HALF = 640
WIDE = 1280
FACES = 4
CHARS = (
    ((1, 2, 1.0), (2, 1, -1.0)),
    ((1, 2, -1.0), (2, 1, 1.0)),
    ((0, 2, -1.0), (2, 0, 1.0)),
    ((0, 2, 1.0), (2, 0, -1.0)),
)
SIDES = ((0, 4, 0), (0, 0, 4), (1, 4, 0), (1, 0, 4))


def lobatto_scaled():
    radical = math.sqrt(3.0 / 7.0)
    points = np.array([-1.0, -radical, 0.0, radical, 1.0])
    legendre = (35.0 * points**4 - 30.0 * points**2 + 3.0) / 8.0
    weights = 0.1 / legendre**2
    matrix = np.zeros((5, 5))
    for i in range(5):
        for j in range(5):
            if i != j:
                matrix[i, j] = legendre[i] / (legendre[j] * (points[i] - points[j]))
    root = np.sqrt(weights)
    return matrix * root[:, None] / root[None, :], root


def row_of(comp, i, j):
    return comp * 25 + 5 * i + j


def split_np(matrix):
    high = np.asarray(matrix, np.float32).astype(jnp.bfloat16)
    low = (np.asarray(matrix, np.float32) - high.astype(np.float32)).astype(jnp.bfloat16)
    return high, low


def tables():
    deriv, root = lobatto_scaled()
    deriv = STEP_SIZE * deriv
    curl = np.zeros((ROWS, ROWS))
    turn = np.zeros((QROWS, ROWS))
    for i in range(5):
        for j in range(5):
            for k in range(5):
                curl[row_of(0, i, j), row_of(2, i, k)] += deriv[j, k]
                curl[row_of(1, i, j), row_of(2, k, j)] -= deriv[i, k]
                curl[row_of(2, i, j), row_of(1, k, j)] += deriv[i, k]
                curl[row_of(2, i, j), row_of(0, i, k)] -= deriv[j, k]
            turn[row_of(0, i, j), row_of(1, i, j)] = 1.0
            turn[row_of(1, i, j), row_of(0, i, j)] = -1.0
    high, low = split_np(curl)
    inner = np.zeros((ROWS + 64, 256), jnp.bfloat16)
    inner[:ROWS, 0:80] = high
    inner[:ROWS, 80:160] = high
    inner[:ROWS, 160:240] = low
    inner[ROWS : ROWS + QROWS, 0:80] = turn.astype(jnp.bfloat16)
    inner[ROWS : ROWS + QROWS, 80:160] = turn.astype(jnp.bfloat16)

    send_e = np.zeros((64, 256), jnp.bfloat16)
    send_h = np.zeros((64, 256), jnp.bfloat16)
    lift = np.zeros((2 * ROWS, 128), jnp.bfloat16)
    for face in range(FACES):
        axis, node_out, node_in = SIDES[face]
        for slot in range(16):
            char = slot if slot < 8 else 8 + slot % 2
            which, along = char // 5, char % 5
            comp_e, comp_h, sign = CHARS[face][which]
            spot_out = (node_out, along) if axis == 0 else (along, node_out)
            spot_in = (node_in, along) if axis == 0 else (along, node_in)
            at = face * 16 + slot
            for part in (0, 80):
                send_e[at, part + row_of(comp_e, *spot_out)] = 1.0
                send_h[at, part + row_of(comp_h, *spot_out)] = sign
            for part in (0, 64):
                lift[row_of(comp_e, *spot_in), part + at] = 1.0
                lift[ROWS + row_of(comp_h, *spot_in), part + at] = sign

    columns = np.zeros((5, ROWS), np.float32)
    strength = STEP_SIZE * LIFT_HALF
    for comp in range(3):
        for i in range(5):
            for j in range(5):
                row = row_of(comp, i, j)
                columns[0, row] = root[i] * root[j]
                columns[1, row] = 1.0 / (root[i] * root[j])
                count = (i in (0, 4)) * (comp != 0) + (j in (0, 4)) * (comp != 1)
                columns[2, row] = strength * count
                columns[3, row] = strength * (count + (comp != 2))
                columns[4, row] = strength * (comp != 2)
    spread = np.ascontiguousarray(np.broadcast_to(columns[:, :, None], (5, ROWS, 128)))

    order = np.zeros((HALF, HALF), jnp.bfloat16)
    for z in range(HALF):
        order[z, (z % 5) * 128 + z // 5] = 1.0
    return inner, send_e, send_h, lift, spread, order


def split(value):
    high = value.astype(BF16)
    return high, (value - high.astype(F32)).astype(BF16)


def dot(a, b):
    return jnp.dot(a, b, preferred_element_type=F32)


def dot_nt(a, b):
    return lax.dot_general(a, b, (((1,), (1,)), ((), ())), preferred_element_type=F32)


def lanes(block):
    return slice(block * 128, block * 128 + 128)


def kernel(
    n_gx, n_gy, data_ref, cond_ref, supp_ref, tags_ref, nodes_ref, inner_ref, send_e_ref, send_h_ref, lift_ref,
    spread_ref, order_ref, est_ref, res_ref,
    fields, rates, saved, rhs, prod, ghost_rhs, sig, gain, pick_row, pick_lane, pick_back, left, unit, record,
    source, basis, scalars, perm, send_buf, recv_buf, red_buf, send_sem, recv_sem, red_send_sem, red_recv_sem,
):
    deriv, root = lobatto_scaled()
    deriv = STEP_SIZE * deriv
    gx, gy = lax.axis_index("gx"), lax.axis_index("gy")
    x_at, z_at = lax.rem(gx, NX_CHIPS), lax.div(gx, NX_CHIPS)
    core_at, y_at = lax.rem(gy, CORES), lax.div(gy, CORES)
    n_z, n_y, n_xc = n_gx // NX_CHIPS, n_gy // CORES, NX_CHIPS * CORES
    sizes = (n_xc, n_z, n_y)

    def partner(phase, step):
        if phase == 0:
            spot = lax.rem(x_at * CORES + core_at + step, n_xc)
            return (z_at * NX_CHIPS + lax.div(spot, CORES), y_at * CORES + lax.rem(spot, CORES))
        if phase == 1:
            return (lax.rem(z_at + step, n_z) * NX_CHIPS + x_at, gy)
        return (gx, lax.rem(y_at + step, n_y) * CORES + core_at)

    beside = (
        (lax.rem(gx + 1, n_gx), gy),
        (lax.rem(gx + n_gx - 1, n_gx), gy),
        (gx, lax.rem(gy + 1, n_gy)),
        (gx, lax.rem(gy + n_gy - 1, n_gy)),
    )
    strength = STEP_SIZE * LIFT_HALF
    open_faces = (
        jnp.where(gx > 0, strength, 0.0).astype(F32),
        jnp.where(gx < n_gx - 1, strength, 0.0).astype(F32),
        jnp.where(gy > 0, strength, 0.0).astype(F32),
        jnp.where(gy < n_gy - 1, strength, 0.0).astype(F32),
    )

    barrier = pltpu.get_barrier_semaphore()
    greeted = 0
    for device in beside:
        pl.semaphore_signal(barrier, inc=1, device_id=device, device_id_type=MESH)
        greeted += 1
    for phase in range(3):
        for step in range(1, sizes[phase]):
            pl.semaphore_signal(barrier, inc=1, device_id=partner(phase, step), device_id_type=MESH)
            greeted += 1

    tag_low = tags_ref[0, 0, 0].astype(F32)
    tag_high = tags_ref[1, 0, 0].astype(F32)
    perm[...] = jnp.zeros_like(perm)
    for comp in range(3):
        for i in range(5):
            perm[comp * 25 + i * 5 : comp * 25 + i * 5 + 5, :] = cond_ref[i]
    high, low = split(perm[0:ROWS, :])
    order = order_ref[...]
    for k in range(5):
        both = dot(jnp.concatenate([high, low], axis=0), order_ref[:, lanes(k)])
        own = spread_ref[3 if k in (0, 4) else 2]
        sig[:, lanes(k)] = STEP_SIZE * (both[0:ROWS] + both[ROWS : 2 * ROWS]) + own
    support = supp_ref[0].astype(F32)
    for k in range(5):
        gain[:, lanes(k)] = (-DRIVE_GAIN * STEP_SIZE * float(root[k])) * support * spread_ref[0]

    node = nodes_ref[...].astype(F32)
    pair = jnp.floor((node + 0.5) * (1.0 / HALF))
    depth = node - float(HALF) * pair
    element = jnp.floor((depth + 0.5) * 0.2)
    inside = depth - 5.0 * element
    weight = jnp.zeros_like(node)
    for k in range(5):
        weight = jnp.where(inside == float(k), float(1.0 / root[k]), weight)
    row_id = lax.broadcasted_iota(jnp.int32, (ROWS, 128), 0)
    comp_id = (row_id >= 25).astype(jnp.int32) + (row_id >= 50).astype(jnp.int32) + (row_id >= 75).astype(jnp.int32)
    spot_id = (row_id - 25 * comp_id).astype(F32)
    pick_row[...] = jnp.where(spot_id == pair, spread_ref[1] * weight, 0.0)
    sub_id = lax.broadcasted_iota(jnp.int32, (128, 128), 0).astype(F32)
    for k in range(5):
        hot = jnp.where((sub_id == element) & (inside == float(k)), 1.0, 0.0)
        pick_lane[lanes(k), :] = hot.astype(BF16)
        flipped = jnp.transpose(hot).astype(BF16)
        pick_back[0:128, lanes(k)] = flipped
        pick_back[128:256, lanes(k)] = flipped

    left[...] = jnp.zeros_like(left)
    left[0, 0:3, :] = data_ref[0]
    left[1, 0:3, :] = data_ref[1]
    basis[0] = jnp.zeros_like(basis[0])
    rhs[240:256, :] = jnp.zeros((16, WIDE), BF16)
    sub8 = lax.broadcasted_iota(jnp.int32, (8, 128), 0)
    lane56 = lax.broadcasted_iota(jnp.int32, (QROWS, 128), 1)

    pl.semaphore_wait(barrier, greeted)

    def reduce_send(index, phase, row):
        red_buf[index, phase, 0] = row
        for step in range(1, sizes[phase]):
            pltpu.make_async_remote_copy(
                src_ref=red_buf.at[index, phase, 0],
                dst_ref=red_buf.at[index, phase, step],
                send_sem=red_send_sem.at[index, phase],
                recv_sem=red_recv_sem.at[index, phase],
                device_id=partner(phase, step),
                device_id_type=MESH,
            ).start()

    def reduce_take(index, phase):
        if sizes[phase] == 1:
            return red_buf[index, phase, 0]
        others = red_buf.at[index, phase, pl.ds(1, sizes[phase] - 1)]
        pltpu.make_async_copy(others, others, red_recv_sem.at[index, phase]).wait()
        pltpu.make_async_copy(others, others, red_send_sem.at[index, phase]).wait()
        total = red_buf[index, phase, 0]
        for step in range(1, sizes[phase]):
            total = total + red_buf[index, phase, step]
        return total

    def whole(row):
        return jnp.sum(row, axis=1, keepdims=True)

    def data_squares():
        return jnp.sum(left[0] * left[0] + left[1] * left[1], axis=0, keepdims=True)

    def source_squares():
        total = jnp.zeros((ROWS, 128), F32)
        for moment in range(2):
            for k in range(5):
                piece = source[moment, :, lanes(k)]
                total = total + piece * piece
        return jnp.sum(total, axis=0, keepdims=True)

    def apply_rates(step, hook):
        for block in range(10):
            high, low = split(fields[:, lanes(block)])
            rhs[0:80, lanes(block)] = high
            rhs[80:160, lanes(block)] = low
            rhs[160:240, lanes(block)] = high
        out = dot(send_e_ref[...], rhs[:, 0:HALF]) + dot(send_h_ref[...], rhs[:, HALF:WIDE])
        copies = []
        for face in range(FACES):
            base = face * 16
            packed = jnp.zeros((8, 128), F32)
            for k in range(5):
                send_buf[step, face, 8 * k : 8 * k + 8, :] = out[base : base + 8, lanes(k)]
                if k < 4:
                    packed = jnp.where((sub8 >= 2 * k) & (sub8 < 2 * k + 2), out[base + 8 : base + 16, lanes(k)], packed)
            send_buf[step, face, 40:48, :] = packed
            send_buf[step, face, 48:56, :] = out[base + 8 : base + 16, lanes(4)]
            copy = pltpu.make_async_remote_copy(
                src_ref=send_buf.at[step, face],
                dst_ref=recv_buf.at[step, face],
                send_sem=send_sem.at[step, face],
                recv_sem=recv_sem.at[step, face],
                device_id=beside[face],
                device_id_type=MESH,
            )
            copy.start()
            copies.append(copy)

        hook()
        prod[...] = dot(inner_ref[...], rhs[...])
        for half in range(2):
            own0, other0 = half * 5, (1 - half) * 5
            sign = 1.0 if half == 0 else -1.0
            for k in range(5):
                slope = None
                for m in range(5):
                    if m != k and abs(deriv[k, m]) > 1e-12:
                        term = float(deriv[k, m]) * prod[80:136, lanes(other0 + m)]
                        slope = term if slope is None else slope + term
                decay = sig[:, lanes(k)] if half == 0 else spread_ref[3 if k in (0, 4) else 2]
                change = sign * prod[0:80, lanes(other0 + k)] - decay * fields[:, lanes(own0 + k)]
                upper = change[0:QROWS] - sign * slope
                if k in (0, 4):
                    own_low, turn_low = fields[0:QROWS, lanes(own0)], prod[80:136, lanes(other0)]
                    own_high, turn_high = fields[0:QROWS, lanes(own0 + 4)], prod[80:136, lanes(other0 + 4)]
                    if half == 1:
                        turn_low, turn_high = -turn_low, -turn_high
                    if k == 0:
                        inward = pltpu.roll(own_high + turn_high, 1, 1)
                        edge = (tag_low * -sign) * (own_low - turn_low)
                        incoming = jnp.where(lane56 == 0, edge, inward)
                    else:
                        inward = pltpu.roll(own_low - turn_low, 127, 1)
                        edge = (tag_high * -sign) * (own_high + turn_high)
                        incoming = jnp.where(lane56 == 127, edge, inward)
                    upper = upper + spread_ref[4][0:QROWS] * incoming
                rates[0:QROWS, lanes(own0 + k)] = upper
                rates[QROWS:ROWS, lanes(own0 + k)] = change[QROWS:ROWS]

        for copy in copies:
            copy.wait()
        for face in range(FACES):
            for k in range(5):
                packed = recv_buf[step, face, 40:48, :] if k < 4 else recv_buf[step, face, 48:56, :]
                start = 2 * k if k < 4 else 0
                packed = jnp.where((sub8 >= start) & (sub8 < start + 2), packed, 0.0)
                piece = jnp.concatenate([recv_buf[step, face, 8 * k : 8 * k + 8, :], packed], axis=0)
                high, low = split(open_faces[face] * piece)
                ghost_rhs[face * 16 : face * 16 + 16, lanes(k)] = high
                ghost_rhs[64 + face * 16 : 64 + face * 16 + 16, lanes(k)] = low
        lifted = dot(lift_ref[...], ghost_rhs[...])
        rates[:, 0:HALF] += lifted[0:ROWS]
        rates[:, HALF:WIDE] += lifted[ROWS : 2 * ROWS]

    def inject(moment):
        values = jnp.where(
            comp_id == 0, left[moment, 0:1, :], jnp.where(comp_id == 1, left[moment, 1:2, :], left[moment, 2:3, :])
        )
        high, low = split(pick_row[...] * values)
        return dot(jnp.concatenate([high, low], axis=1), pick_back[...])

    def gather(halves, moment):
        both = dot(halves, pick_lane[...])
        chosen = (both[0:ROWS] + both[ROWS : 2 * ROWS]) * pick_row[...]
        out = jnp.zeros((8, 128), F32)
        for comp in range(3):
            part = jnp.sum(jnp.where(comp_id == comp, chosen, 0.0), axis=0, keepdims=True)
            out = jnp.where(sub8 == comp, part, out)
        record[moment] = out

    def nothing():
        pass

    def sweep(turn, carry):
        first = turn * 6
        data_red, source_red = turn * 2, turn * 2 + 1

        fields[:, 0:HALF] = inject(1)
        fields[:, HALF:WIDE] = jnp.zeros((ROWS, HALF), F32)
        apply_rates(first, lambda: reduce_send(data_red, 0, data_squares()))
        for k in range(5):
            source[1, :, lanes(k)] = gain[:, lanes(k)] * (fields[:, lanes(k)] + 0.5 * rates[:, lanes(k)])
        for block in range(10):
            piece = rates[:, lanes(block)]
            saved[:, lanes(block)] = fields[:, lanes(block)] + piece
            fields[:, lanes(block)] = piece

        def second():
            reduce_send(data_red, 1, reduce_take(data_red, 0))

        apply_rates(first + 1, second)
        fields[:, 0:HALF] = inject(0) + saved[:, 0:HALF] + 0.5 * rates[:, 0:HALF]
        fields[:, HALF:WIDE] = saved[:, HALF:WIDE] + 0.5 * rates[:, HALF:WIDE]

        def third():
            reduce_send(data_red, 2, reduce_take(data_red, 1))

        apply_rates(first + 2, third)
        beta = jnp.sqrt(whole(reduce_take(data_red, 2)))
        inverse = 1.0 / beta
        scalars[turn, 0] = jnp.broadcast_to(beta, (8, 128))
        for k in range(5):
            part = gain[:, lanes(k)] * (fields[:, lanes(k)] + 0.5 * rates[:, lanes(k)])
            part = part * inverse - beta * basis[turn, 0, :, lanes(k)]
            source[0, :, lanes(k)] = part
            source[1, :, lanes(k)] = source[1, :, lanes(k)] * inverse - beta * basis[turn, 1, :, lanes(k)]
            fields[:, lanes(k)] = gain[:, lanes(k)] * part
        fields[:, HALF:WIDE] = jnp.zeros((ROWS, HALF), F32)
        unit[...] = left[...] * inverse

        apply_rates(first + 3, lambda: reduce_send(source_red, 0, source_squares()))
        for block in range(10):
            fields[:, lanes(block)] = fields[:, lanes(block)] + 0.5 * rates[:, lanes(block)]

        def fifth():
            gather(rhs[0:160, 0:HALF], 0)
            reduce_send(source_red, 1, reduce_take(source_red, 0))

        apply_rates(first + 4, fifth)
        for k in range(5):
            drive = gain[:, lanes(k)] * source[1, :, lanes(k)]
            start = fields[:, lanes(k)]
            saved[:, lanes(k)] = start + drive
            fields[:, lanes(k)] = start + 0.5 * (rates[:, lanes(k)] + drive)
            fields[:, lanes(5 + k)] = fields[:, lanes(5 + k)] + 0.5 * rates[:, lanes(5 + k)]

        def sixth():
            reduce_send(source_red, 2, reduce_take(source_red, 1))

        apply_rates(first + 5, sixth)
        halves = split(saved[:, 0:HALF] + rates[:, 0:HALF])
        gather(jnp.concatenate(halves, axis=0), 1)
        alpha = jnp.sqrt(whole(reduce_take(source_red, 2)))
        scalars[turn, 1] = jnp.broadcast_to(alpha, (8, 128))
        inverse = 1.0 / alpha
        for moment in range(2):
            basis[turn + 1, moment] = source[moment] * inverse
            left[moment] = record[moment] * inverse - alpha * unit[moment]
        return carry

    lax.fori_loop(0, 2, sweep, 0)

    reduce_send(4, 0, data_squares())
    for turn in range(2):
        for moment in range(2):
            high, low = split(basis[turn + 1, moment])
            both = dot_nt(jnp.concatenate([high, low], axis=0), order)
            perm[(turn * 2 + moment) * ROWS : (turn * 2 + moment + 1) * ROWS, :] = both[0:ROWS] + both[ROWS : 2 * ROWS]
    reduce_send(4, 1, reduce_take(4, 0))
    reduce_send(4, 2, reduce_take(4, 1))
    beta_3 = jnp.sqrt(whole(reduce_take(4, 2)))
    beta_1, alpha_1 = scalars[0, 0][0:1, :], scalars[0, 1][0:1, :]
    beta_2, alpha_2 = scalars[1, 0][0:1, :], scalars[1, 1][0:1, :]
    rho_1 = jnp.sqrt(alpha_1 * alpha_1 + beta_2 * beta_2)
    cosine, sine = alpha_1 / rho_1, beta_2 / rho_1
    step_1 = cosine * beta_1 / rho_1
    phi_bar = sine * beta_1
    theta = sine * alpha_2
    rho_bar = -cosine * alpha_2
    rho_2 = jnp.sqrt(rho_bar * rho_bar + beta_3 * beta_3)
    step_2 = rho_bar / rho_2 * phi_bar / rho_2
    use_1 = (step_1 - step_2 * theta / rho_1)[:, 0:1]
    use_2 = step_2[:, 0:1]
    use_left = (phi_bar / rho_2)[:, 0:1]
    for moment in range(2):
        res_ref[moment] = (left[moment] * use_left)[0:3, :]
        for comp in range(3):
            for i in range(5):
                at = comp * 25 + i * 5
                one = perm[moment * ROWS + at : moment * ROWS + at + 5, :]
                two = perm[(2 + moment) * ROWS + at : (2 + moment) * ROWS + at + 5, :]
                est_ref[moment, comp, i] = use_1 * one + use_2 * two


def solution(mesh):
    n_gx, n_gy = mesh.shape["gx"], mesh.shape["gy"]
    inner, send_e, send_h, lift, spread, order = tables()

    def shards(probe_data, conductivity, support, face_tags, probe_nodes):
        vmem = pl.BlockSpec(memory_space=pltpu.VMEM)
        smem = pl.BlockSpec(memory_space=pltpu.SMEM)
        return pl.pallas_call(
            functools.partial(kernel, n_gx, n_gy),
            out_shape=(
                jax.ShapeDtypeStruct((2, 3, 5, 5, HALF), F32),
                jax.ShapeDtypeStruct((2, 3, 128), F32),
            ),
            in_specs=[vmem, vmem, vmem, smem] + [vmem] * 7,
            out_specs=(vmem, vmem),
            scratch_shapes=[
                pltpu.VMEM((ROWS, WIDE), F32),
                pltpu.VMEM((ROWS, WIDE), F32),
                pltpu.VMEM((ROWS, WIDE), F32),
                pltpu.VMEM((256, WIDE), BF16),
                pltpu.VMEM((ROWS + 64, WIDE), F32),
                pltpu.VMEM((128, HALF), BF16),
                pltpu.VMEM((ROWS, HALF), F32),
                pltpu.VMEM((ROWS, HALF), F32),
                pltpu.VMEM((ROWS, 128), F32),
                pltpu.VMEM((HALF, 128), BF16),
                pltpu.VMEM((256, HALF), BF16),
                pltpu.VMEM((2, 8, 128), F32),
                pltpu.VMEM((2, 8, 128), F32),
                pltpu.VMEM((2, 8, 128), F32),
                pltpu.VMEM((2, ROWS, HALF), F32),
                pltpu.VMEM((3, 2, ROWS, HALF), F32),
                pltpu.VMEM((2, 2, 8, 128), F32),
                pltpu.VMEM((4 * ROWS, HALF), F32),
                pltpu.VMEM((12, FACES, QROWS, 128), F32),
                pltpu.VMEM((12, FACES, QROWS, 128), F32),
                pltpu.VMEM((5, 3, 8, 1, 128), F32),
                pltpu.SemaphoreType.DMA((12, FACES)),
                pltpu.SemaphoreType.DMA((12, FACES)),
                pltpu.SemaphoreType.DMA((5, 3)),
                pltpu.SemaphoreType.DMA((5, 3)),
            ],
            compiler_params=pltpu.CompilerParams(
                collective_id=0, has_side_effects=True, vmem_limit_bytes=40 * 1024 * 1024
            ),
        )(
            probe_data, conductivity, support, face_tags, probe_nodes.reshape(1, 128),
            jnp.asarray(inner), jnp.asarray(send_e), jnp.asarray(send_h), jnp.asarray(lift), jnp.asarray(spread),
            jnp.asarray(order),
        )

    return jax.shard_map(
        shards,
        mesh=mesh,
        in_specs=(
            P(None, None, ("gx", "gy")),
            P("gx", "gy", None),
            P("gx", "gy", None),
            P(None, "gx", "gy"),
            P(("gx", "gy")),
        ),
        out_specs=(P(None, None, "gx", "gy", None), P(None, None, ("gx", "gy"))),
        check_vma=False,
    )
```

time: 1070 us -> 99.4 us (0.09); the launches traced: 1060 us -> 98.6 us
  blocking collectives: 538 us -> 0 us
  local copies, waits for them, and re-layouts: 181 us -> 9.07 us
  other arithmetic: 146 us -> 0 us
  starting transfers between devices: 141 us -> 0 us
  Pallas kernels: 0 us -> 88.9 us
  waiting for transfers between devices: 39 us -> 0 us
    psum x5 -> x0, blocking collectives: 538 us -> none  [the longest x3 321 us: data_norm(): return jnp.sqrt(lax.psum(jnp.sum(vector * vector), ('gx', 'gy')))]
    ppermute x48 -> x0, starting transfers between devices: 141 us -> none  [the longest x24 98.7 us: with_halo(): before = lax.ppermute(last, axis, up)]
    pallas_call x0 -> x1, Pallas kernels: none -> 88.9 us  [shards(): pl.pallas_call(functools.partial(kernel, n_gx, n_gy), out_shape=(jax.Shap...]
    another operation x66 -> x0, local copies, waits for them, and re-layouts: 68.5 us -> none  [the longest x15 44.2 us: evaluate(): jnp.stack([curl_h[0] - conduct * fields[0], curl_h[1] - conduct * fields[...]
    ppermute x48 -> x0, waiting for transfers between devices: 39 us -> none  [the longest x24 24.8 us: with_halo(): after = lax.ppermute(leading, axis, down)]
    add x7 -> x0, local copies, waits for them, and re-layouts: 32.2 us -> none  [the longest x5 25.2 us: adjoint(): carried.at[0:3].add(injected.reshape(3, rows_x, rows_y, depth_nodes))]
    slice x34 -> x0, local copies, waits for them, and re-layouts: 30.3 us -> none  [the longest x4 22.1 us: shards(): forward_fields[0:3].reshape(3, node_count)]
    mul x171 -> x0, other arithmetic: 28.1 us -> none  [the longest x36 10.6 us: apply_lobatto(): term = weight * lax.index_in_dim(blocks, col_idx, node_axis, keepdims=False)]
  transfers between devices with their start and end apart: 48 -> 0, of which waited for: 16 -> 0; matrix products, arithmetic and copies ran while one was open for 10% -> 0% of each run, Pallas kernels for 0% -> 0%
where the time goes in v1:
time: 99.4 us; the launch traced here: 98.6 us
  Pallas kernels  88.9 us (89%)
  local copies, waits for them, and re-layouts  9.07 us (9%)
    pallas_call x1, Pallas kernels, shards(): pl.pallas_call(functools.partial(kernel, n_gx, n_gy), out_shape=(jax.Shap...  88.9 us
    unnamed x24, local copies, waits for them, and re-layouts  7.55 us

profile of v1, /device:TPU:1, one launch (start us, length us, event | category | flops | bytes accessed | tf_op | source)
XLA Modules:
  0.0 98.6 jit_solution(839954326823641718)
XLA Ops:
  0.6 0.0 copy-start.10
  0.6 0.0 copy-start.9
  0.6 0.6 copy-done.10
  1.3 0.1 copy.14.tags_ref
  1.4 0.0 copy-done.9
  1.4 0.0 copy-start.7
  1.4 0.0 copy-start.8
  1.4 0.6 copy-done.7
  2.0 0.0 copy-done.8
  2.1 0.0 copy-start
  2.1 1.1 %copy-done = bf16[640,640]{1,0:T(8,128)(2,1)S(1)} copy-done((bf16[640,640]{1,0:T(8,128)(2,1)S(1)}, bf16[640,640]{1,0:T(8,128)(2,1)}, u32[]{:S(2)}) %copy-start) | copy-done | bytes 819224
  3.2 0.0 copy-start.1
  3.2 0.9 copy-done.1
  4.1 0.9 copy-done.2
  5.0 0.0 copy-start.3
  5.0 0.9 copy-done.3
  5.9 0.0 copy-start.4
  5.9 0.8 copy-done.4
  6.7 0.0 copy-start.5
  6.7 0.8 copy-done.5
  7.4 0.8 copy-done.6
  8.2 88.9 %shard_map.122 = (f32[2,3,5,5,640]{4,3,2,1,0:T(8,128)S(1)}, f32[2,3,128]{2,1,0:T(4,128)S(1)}) custom-call(f32[2,3,128]{2,1,0:T(4,128)S(1)} %copy.13.data_ref, f32[5,5,640]{2,1,0:T(8,128)S(1)} %copy-done.2, s32[1,1,128]{2,1,0:T(1,128)S(1)} %copy-done.7, s32[2,1,1]{2,1,0:T(1,128)S(1)} %copy.14.tags_ref, s32[1,128]{1,0:T(1,128)S(1)} %bitcast.1, ...), custom_call_target="tpu_custom_call" | custom-call | tf_op jit(solution)/shard_map/pallas_call | solution.py:467
  97.1 0.9 copy.15
  98.0 0.6 copy.16
  (3 shorter events, 0.0 us)
Async XLA Ops:
  0.6 0.7 copy-start.10
  0.6 0.7 copy-start.9
  1.4 0.7 copy-start.7
  1.4 0.7 copy-start.8
  2.1 1.1 %copy-start = (bf16[640,640]{1,0:T(8,128)(2,1)S(1)}, bf16[640,640]{1,0:T(8,128)(2,1)}, u32[]{:S(2)}) copy-start(bf16[640,640]{1,0:T(8,128)(2,1)} %constant.17.clone.order_ref) | copy-start | bytes 2457604
  3.2 0.9 copy-start.1
  4.1 0.9 copy-start.2
  5.0 0.9 copy-start.3
  5.9 0.8 copy-start.4
  6.7 0.8 copy-start.5
  7.4 0.8 copy-start.6

commit v2 on v1

v2 whole, which is shorter than its diff:
```python
import functools
import math

import jax
import jax.numpy as jnp
import numpy as np
from jax import lax
from jax.experimental import pallas as pl
from jax.experimental.pallas import tpu as pltpu
from jax.sharding import PartitionSpec as P

MESH = pl.DeviceIdType.MESH
F32 = jnp.float32
BF16 = jnp.bfloat16

STEP_SIZE = 0.02
LIFT_HALF = 5.0
DRIVE_GAIN = 50.0
NX_CHIPS = 4
CORES = 2
ROWS = 80
QROWS = 56
HALF = 640
WIDE = 1280
INNER = 144
SENT = 96
FACES = 4
DIAGS = ((-1, -1), (-1, 1), (1, -1), (1, 1))
CHARS = (
    ((1, 2, 1.0), (2, 1, -1.0)),
    ((1, 2, -1.0), (2, 1, 1.0)),
    ((0, 2, -1.0), (2, 0, 1.0)),
    ((0, 2, 1.0), (2, 0, -1.0)),
)
SIDES = ((0, 4, 0), (0, 0, 4), (1, 4, 0), (1, 0, 4))


def lobatto_scaled():
    radical = math.sqrt(3.0 / 7.0)
    points = np.array([-1.0, -radical, 0.0, radical, 1.0])
    legendre = (35.0 * points**4 - 30.0 * points**2 + 3.0) / 8.0
    weights = 0.1 / legendre**2
    matrix = np.zeros((5, 5))
    for i in range(5):
        for j in range(5):
            if i != j:
                matrix[i, j] = legendre[i] / (legendre[j] * (points[i] - points[j]))
    root = np.sqrt(weights)
    return matrix * root[:, None] / root[None, :], root


def row_of(comp, i, j):
    return comp * 25 + 5 * i + j


def split_np(matrix):
    high = np.asarray(matrix, np.float32).astype(jnp.bfloat16)
    low = (np.asarray(matrix, np.float32) - high.astype(np.float32)).astype(jnp.bfloat16)
    return high, low


def tables():
    deriv, root = lobatto_scaled()
    deriv = STEP_SIZE * deriv
    curl = np.zeros((ROWS, ROWS))
    turn = np.zeros((QROWS, ROWS))
    for i in range(5):
        for j in range(5):
            for k in range(5):
                curl[row_of(0, i, j), row_of(2, i, k)] += deriv[j, k]
                curl[row_of(1, i, j), row_of(2, k, j)] -= deriv[i, k]
                curl[row_of(2, i, j), row_of(1, k, j)] += deriv[i, k]
                curl[row_of(2, i, j), row_of(0, i, k)] -= deriv[j, k]
            turn[row_of(0, i, j), row_of(1, i, j)] = 1.0
            turn[row_of(1, i, j), row_of(0, i, j)] = -1.0
    high, low = split_np(curl)
    inner = np.zeros((INNER, 256), np.float32)
    inner[:ROWS, 0:80] = high
    inner[:ROWS, 80:160] = high
    inner[:ROWS, 160:240] = low
    inner[ROWS : ROWS + QROWS, 0:80] = turn
    inner[ROWS : ROWS + QROWS, 80:160] = turn

    send_e = np.zeros((SENT, 256), np.float32)
    send_h = np.zeros((SENT, 256), np.float32)
    lift = np.zeros((2 * ROWS, 256), np.float32)
    corner = np.zeros((128, 256), np.float32)
    slot_weight = np.zeros(64)
    for face in range(FACES):
        axis, node_out, node_in = SIDES[face]
        for slot in range(16):
            char = slot if slot < 8 else 8 + slot % 2
            which, along = char // 5, char % 5
            comp_e, comp_h, sign = CHARS[face][which]
            spot_out = (node_out, along) if axis == 0 else (along, node_out)
            spot_in = (node_in, along) if axis == 0 else (along, node_in)
            at = face * 16 + slot
            slot_weight[at] = root[0] ** 2 * root[along] ** 2
            for part in (0, 80):
                send_e[at, part + row_of(comp_e, *spot_out)] = 1.0
                send_h[at, part + row_of(comp_h, *spot_out)] = sign
            for part in (0, 64):
                lift[row_of(comp_e, *spot_in), part + at] = 1.0
                lift[ROWS + row_of(comp_h, *spot_in), part + at] = sign
            for diag, (side_x, side_y) in enumerate(DIAGS):
                if axis == 0:
                    if side_x != (-1 if face == 0 else 1):
                        continue
                    other, first = (2 if side_y < 0 else 3), 2
                else:
                    if side_y != (-1 if face == 2 else 1):
                        continue
                    other, first = (0 if side_x < 0 else 1), 0
                if along != SIDES[other][2]:
                    continue
                for number, (other_e, other_h, other_sign) in enumerate(CHARS[other]):
                    only_e = float(comp_e == other_e)
                    both = only_e + sign * other_sign * float(comp_h == other_h)
                    for part in (0, 4, 32, 36):
                        column = diag * 8 + first + number + part
                        corner[at, column] = both
                        corner[64 + at, column] = only_e
    for diag, (side_x, side_y) in enumerate(DIAGS):
        spot = (4 if side_x < 0 else 0, 4 if side_y < 0 else 0)
        for slot in range(8):
            face = ((0 if side_x < 0 else 1), (2 if side_y < 0 else 3))[slot % 4 // 2]
            comp_e, comp_h, sign = CHARS[face][slot % 2]
            for part in (0, 80):
                send_e[64 + diag * 8 + slot, part + row_of(comp_e, *spot)] = 1.0
                send_h[64 + diag * 8 + slot, part + row_of(comp_h, *spot)] = sign
    matrices = np.concatenate([inner, send_e, send_h, lift, corner], axis=0)

    columns = np.zeros((ROWS, 128), np.float32)
    strength = STEP_SIZE * LIFT_HALF
    for comp in range(3):
        for i in range(5):
            for j in range(5):
                row = row_of(comp, i, j)
                columns[row, 0] = root[i] * root[j]
                columns[row, 1] = 1.0 / (root[i] * root[j])
                count = (i in (0, 4)) * (comp != 0) + (j in (0, 4)) * (comp != 1)
                columns[row, 2] = strength * count
                columns[row, 3] = strength * (count + (comp != 2))
                columns[row, 4] = strength * (comp != 2)
    columns[0:64, 5] = (DRIVE_GAIN * STEP_SIZE) ** 2 * slot_weight
    return matrices, columns


def split(value):
    high = value.astype(BF16)
    return high, (value - high.astype(F32)).astype(BF16)


def dot(a, b):
    return jnp.dot(a, b, preferred_element_type=F32)


def dot_nt(a, b):
    return lax.dot_general(a, b, (((1,), (1,)), ((), ())), preferred_element_type=F32)


def lanes(block):
    return slice(block * 128, block * 128 + 128)


def kernel(
    n_gx, n_gy, tags_ref, data_hbm, cond_hbm, supp_hbm, nodes_hbm, mats_hbm, cols_hbm, est_ref, res_ref,
    data_ref, cond_ref, supp_ref, nodes_ref, mats_ref, cols_ref, mats, order, spread,
    fields, second, rates, rhs, prod, ghost_rhs, corner_rhs, sig, gain, gain_out, pick_row, pick_lane, pick_back,
    left, source, ortho, perm, perm_out, beside_support,
    send_buf, recv_buf, send_next, recv_next, send_diag, recv_diag, red_buf,
    load_sem, send_sem, recv_sem, next_send_sem, next_recv_sem, diag_send_sem, diag_recv_sem, red_send_sem, red_recv_sem,
    supp_send_sem, supp_recv_sem,
):
    loads = []
    pairs = (
        (data_hbm, data_ref), (nodes_hbm, nodes_ref), (mats_hbm, mats_ref), (cols_hbm, cols_ref),
        (cond_hbm, cond_ref), (supp_hbm, supp_ref),
    )
    for number, (far, near) in enumerate(pairs):
        load = pltpu.make_async_copy(far, near, load_sem.at[number])
        load.start()
        loads.append(load)

    deriv, root = lobatto_scaled()
    deriv = STEP_SIZE * deriv
    gx, gy = lax.axis_index("gx"), lax.axis_index("gy")
    x_at, z_at = lax.rem(gx, NX_CHIPS), lax.div(gx, NX_CHIPS)
    core_at, y_at = lax.rem(gy, CORES), lax.div(gy, CORES)
    n_z, n_y, n_xc = n_gx // NX_CHIPS, n_gy // CORES, NX_CHIPS * CORES
    sizes = (n_xc, n_z, n_y)

    def partner(phase, step):
        if phase == 0:
            spot = lax.rem(x_at * CORES + core_at + step, n_xc)
            return (z_at * NX_CHIPS + lax.div(spot, CORES), y_at * CORES + lax.rem(spot, CORES))
        if phase == 1:
            return (lax.rem(z_at + step, n_z) * NX_CHIPS + x_at, gy)
        return (gx, lax.rem(y_at + step, n_y) * CORES + core_at)

    def near_by(step_x, step_y):
        return (lax.rem(gx + n_gx + step_x, n_gx), lax.rem(gy + n_gy + step_y, n_gy))

    beside = (near_by(1, 0), near_by(-1, 0), near_by(0, 1), near_by(0, -1))
    across = tuple(near_by(-side_x, -side_y) for side_x, side_y in DIAGS)
    strength = STEP_SIZE * LIFT_HALF
    has = {(0, -1): gx > 0, (0, 1): gx < n_gx - 1, (1, -1): gy > 0, (1, 1): gy < n_gy - 1}
    open_faces = tuple(
        jnp.where(has[key], strength, 0.0).astype(F32) for key in ((0, -1), (0, 1), (1, -1), (1, 1))
    )
    open_diags = tuple(
        jnp.where(has[(0, side_x)] & has[(1, side_y)], strength, 0.0).astype(F32) for side_x, side_y in DIAGS
    )

    barrier = pltpu.get_barrier_semaphore()
    greeted = 0
    for device in beside + across:
        pl.semaphore_signal(barrier, inc=1, device_id=device, device_id_type=MESH)
        greeted += 1
    for phase in range(3):
        for step in range(1, sizes[phase]):
            pl.semaphore_signal(barrier, inc=1, device_id=partner(phase, step), device_id_type=MESH)
            greeted += 1

    def remote(src, dst, sem_out, sem_in, device):
        copy = pltpu.make_async_remote_copy(
            src_ref=src, dst_ref=dst, send_sem=sem_out, recv_sem=sem_in, device_id=device, device_id_type=MESH
        )
        copy.start()
        return copy

    z_id = lax.broadcasted_iota(jnp.int32, (HALF, 128), 0)
    five = 5 * lax.broadcasted_iota(jnp.int32, (HALF, 128), 1)
    for k in range(5):
        order[:, lanes(k)] = jnp.where(z_id == five + k, 1.0, 0.0).astype(BF16)
    rhs[240:256, :] = jnp.zeros((16, WIDE), BF16)
    left[...] = jnp.zeros_like(left)
    perm[...] = jnp.zeros_like(perm)
    sub8 = lax.broadcasted_iota(jnp.int32, (8, 128), 0)
    lane56 = lax.broadcasted_iota(jnp.int32, (QROWS, 128), 1)
    lane1 = lax.broadcasted_iota(jnp.int32, (1, 128), 1)
    row_id = lax.broadcasted_iota(jnp.int32, (ROWS, 128), 0)
    comp_id = (row_id >= 25).astype(jnp.int32) + (row_id >= 50).astype(jnp.int32) + (row_id >= 75).astype(jnp.int32)
    spot_id = (row_id - 25 * comp_id).astype(F32)

    for load in loads:
        load.wait()
    mats[...] = mats_ref[...].astype(BF16)
    at_e, at_h, at_lift, at_corner = INNER, INNER + SENT, INNER + 2 * SENT, INNER + 2 * SENT + 2 * ROWS
    inner = mats.at[0:INNER]
    send_e, send_h = mats.at[at_e:at_h], mats.at[at_h:at_lift]
    lift = mats.at[at_lift:at_corner, 0:128]
    for number in range(3):
        spread[number] = jnp.broadcast_to(cols_ref[:, 2 + number : 3 + number], (ROWS, 128))

    node = nodes_ref[...].astype(F32)
    pair = jnp.floor((node + 0.5) * (1.0 / HALF))
    depth = node - float(HALF) * pair
    element = jnp.floor((depth + 0.5) * 0.2)
    inside = depth - 5.0 * element
    weight = jnp.zeros_like(node)
    for k in range(5):
        weight = jnp.where(inside == float(k), float(1.0 / root[k]), weight)
    pick_row[...] = jnp.where(spot_id == pair, cols_ref[:, 1:2] * weight, 0.0)
    sub_id = lax.broadcasted_iota(jnp.int32, (128, 128), 0).astype(F32)
    for k in range(5):
        hot = jnp.where((sub_id == element) & (inside == float(k)), 1.0, 0.0)
        pick_lane[lanes(k), :] = hot.astype(BF16)
        flipped = jnp.transpose(hot).astype(BF16)
        pick_back[0:128, lanes(k)] = flipped
        pick_back[128:256, lanes(k)] = flipped
    for comp in range(3):
        for moment in range(2):
            left[0, moment, comp : comp + 1, :] = data_ref[comp, moment : moment + 1, :]

    tag_low = tags_ref[0, 0, 0].astype(F32)
    tag_high = tags_ref[0, 0, 1].astype(F32)
    for comp in range(3):
        for i in range(5):
            perm[comp * 25 + i * 5 : comp * 25 + i * 5 + 5, :] = cond_ref[i]
    halves = jnp.concatenate(split(perm[0:ROWS, :]), axis=0)
    for k in range(5):
        both = dot(halves, order[:, lanes(k)])
        sig[:, lanes(k)] = STEP_SIZE * (both[0:ROWS] + both[ROWS : 2 * ROWS]) + spread[1 if k in (0, 4) else 0]
    support = supp_ref[0].astype(F32)
    for k in range(5):
        gain[:, lanes(k)] = (-DRIVE_GAIN * STEP_SIZE * float(root[k])) * support * cols_ref[:, 0:1]
    beside_support[4] = support

    pl.semaphore_wait(barrier, greeted)
    support_copies = [
        remote(
            beside_support.at[4], beside_support.at[face], supp_send_sem.at[face], supp_recv_sem.at[face], beside[face]
        )
        for face in range(FACES)
    ]

    def reduce_send(index, phase, row):
        red_buf[index, phase, 0] = row
        for step in range(1, sizes[phase]):
            remote(
                red_buf.at[index, phase, 0], red_buf.at[index, phase, step], red_send_sem.at[index, phase],
                red_recv_sem.at[index, phase], partner(phase, step),
            )

    def reduce_take(index, phase):
        if sizes[phase] == 1:
            return red_buf[index, phase, 0]
        others = red_buf.at[index, phase, pl.ds(1, sizes[phase] - 1)]
        pltpu.make_async_copy(others, others, red_recv_sem.at[index, phase]).wait()
        pltpu.make_async_copy(others, others, red_send_sem.at[index, phase]).wait()
        total = red_buf[index, phase, 0]
        for step in range(1, sizes[phase]):
            total = total + red_buf[index, phase, step]
        return total

    def whole(value):
        return jnp.sum(jnp.sum(value, axis=0, keepdims=True), axis=1, keepdims=True)

    def packed_row(values):
        row = jnp.zeros((1, 128), F32)
        for number, value in enumerate(values):
            row = jnp.where(lane1 == number, value, row)
        return row

    def entry(row, number):
        return jnp.sum(jnp.where(lane1 == number, row, 0.0), axis=1, keepdims=True)

    def data_dot(a, b):
        return whole(a[0] * b[0] + a[1] * b[1])

    def source_dot(a, b):
        total = jnp.zeros((ROWS, 128), F32)
        for moment in range(2):
            for k in range(5):
                total = total + a[moment, :, lanes(k)] * b[moment, :, lanes(k)]
        return whole(total)

    def load_rhs(ref, blocks=10):
        for block in range(blocks):
            high, low = split(ref[:, lanes(block)])
            rhs[0:80, lanes(block)] = high
            rhs[80:160, lanes(block)] = low
            rhs[160:240, lanes(block)] = high

    def own_rates(field, result, halves):
        if len(halves) == 2:
            prod[...] = dot(inner[...], rhs[...])
        else:
            prod[:, HALF:WIDE] = dot(inner[...], rhs[:, HALF:WIDE])
        for half in halves:
            own0, other0 = half * 5, (1 - half) * 5
            sign = 1.0 if half == 0 else -1.0
            for k in range(5):
                slope = None
                for m in range(5):
                    if m != k and abs(deriv[k, m]) > 1e-12:
                        term = float(deriv[k, m]) * prod[80:136, lanes(other0 + m)]
                        slope = term if slope is None else slope + term
                decay = sig[:, lanes(k)] if half == 0 else spread[1 if k in (0, 4) else 0]
                change = sign * prod[0:80, lanes(other0 + k)] - decay * field[:, lanes(own0 + k)]
                upper = change[0:QROWS] - sign * slope
                if k in (0, 4):
                    own_low, turn_low = field[0:QROWS, lanes(own0)], prod[80:136, lanes(other0)]
                    own_high, turn_high = field[0:QROWS, lanes(own0 + 4)], prod[80:136, lanes(other0 + 4)]
                    if half == 1:
                        turn_low, turn_high = -turn_low, -turn_high
                    if k == 0:
                        inward = pltpu.roll(own_high + turn_high, 1, 1)
                        edge = (tag_low * -sign) * (own_low - turn_low)
                        incoming = jnp.where(lane56 == 0, edge, inward)
                    else:
                        inward = pltpu.roll(own_low - turn_low, 127, 1)
                        edge = (tag_high * -sign) * (own_high + turn_high)
                        incoming = jnp.where(lane56 == 127, edge, inward)
                    upper = upper + spread[2][0:QROWS] * incoming
                result[0:QROWS, lanes(own0 + k)] = upper
                result[QROWS:ROWS, lanes(own0 + k)] = change[QROWS:ROWS]

    def pack_face(out, face, buf):
        base = face * 16
        mixed = jnp.zeros((8, 128), F32)
        for k in range(5):
            buf[8 * k : 8 * k + 8, :] = out[base : base + 8, lanes(k)]
            if k < 4:
                mixed = jnp.where((sub8 >= 2 * k) & (sub8 < 2 * k + 2), out[base + 8 : base + 16, lanes(k)], mixed)
        buf[40:48, :] = mixed
        buf[48:56, :] = out[base + 8 : base + 16, lanes(4)]

    def kept(k):
        start = 2 * k if k < 4 else 0
        return (sub8 >= start) & (sub8 < start + 2)

    def unpack_face(buf, k):
        mixed = buf[40:48, :] if k < 4 else buf[48:56, :]
        return jnp.concatenate([buf[8 * k : 8 * k + 8, :], jnp.where(kept(k), mixed, 0.0)], axis=0)

    def set_ghosts(face, k, piece):
        high, low = split(open_faces[face] * piece)
        ghost_rhs[face * 16 : face * 16 + 16, lanes(k)] = high
        ghost_rhs[64 + face * 16 : 64 + face * 16 + 16, lanes(k)] = low

    def stage(slot, early, make_second, late, merge, halves_1, halves_2, masked, share):
        load_rhs(fields)
        out = dot(send_e[...], rhs[:, 0:HALF]) + dot(send_h[...], rhs[:, HALF:WIDE])
        copies = []
        for face in range(FACES):
            pack_face(out, face, send_buf.at[slot, face])
            copies.append(
                remote(
                    send_buf.at[slot, face], recv_buf.at[slot, face], send_sem.at[slot, face], recv_sem.at[slot, face],
                    beside[face],
                )
            )
        corner_copies = []
        for diag in range(4):
            base = 64 + diag * 8
            for tile in range(3):
                piece = out[base : base + 8, lanes(2 * tile)]
                if tile < 2:
                    piece = jnp.where(sub8 < 4, piece, out[base : base + 8, lanes(2 * tile + 1)])
                send_diag[slot, diag, 8 * tile : 8 * tile + 8, :] = piece
            corner_copies.append(
                remote(
                    send_diag.at[slot, diag], recv_diag.at[slot, diag], diag_send_sem.at[slot, diag],
                    diag_recv_sem.at[slot, diag], across[diag],
                )
            )
        early()
        own_rates(fields, rates, halves_1)
        make_second()
        load_rhs(second)
        out = dot(send_e[0:64, :], rhs[:, 0:HALF])
        if not masked:
            out = out + dot(send_h[0:64, :], rhs[:, HALF:WIDE])
        next_copies = []
        for face in range(FACES):
            pack_face(out, face, send_next.at[slot, face])
            next_copies.append(
                remote(
                    send_next.at[slot, face], recv_next.at[slot, face], next_send_sem.at[slot, face],
                    next_recv_sem.at[slot, face], beside[face],
                )
            )
        late()

        for copy in copies:
            copy.wait()
        for face in range(FACES):
            for k in range(5):
                set_ghosts(face, k, unpack_face(recv_buf.at[slot, face], k))
        merge(dot(lift[...], ghost_rhs[...]))
        load_rhs(second)
        own_rates(second, rates, halves_2)

        for copy in corner_copies:
            copy.wait()
        for two in range(2):
            for k in range(5):
                pieces = []
                for diag in (2 * two, 2 * two + 1):
                    tile = recv_diag[slot, diag, 8 * (k // 2) : 8 * (k // 2) + 8, :]
                    tile = jnp.where(sub8 >= 4 if k % 2 else sub8 < 4, tile, 0.0)
                    pieces.append(open_diags[diag] * tile)
                high, low = split(jnp.concatenate(pieces, axis=0))
                corner_rhs[16 * two : 16 * two + 16, lanes(k)] = high
                corner_rhs[32 + 16 * two : 32 + 16 * two + 16, lanes(k)] = low
        start = at_corner + (64 if masked else 0)
        extra = dot(mats[start : start + 64, 0:64], corner_rhs[...])
        for copy in next_copies:
            copy.wait()
        for face in range(FACES):
            for k in range(5):
                piece = extra[face * 16 : face * 16 + 16, lanes(k)]
                piece = jnp.concatenate([piece[0:8], jnp.where(kept(k), piece[8:16], 0.0)], axis=0)
                if masked:
                    piece = piece + strength * unpack_face(send_buf.at[slot, face ^ 1], k)
                    piece = piece * gain_out[face * 16 : face * 16 + 16, lanes(k)]
                set_ghosts(face, k, unpack_face(recv_next.at[slot, face], k) + share * piece)
        if len(halves_2) == 2:
            lifted = dot(lift[...], ghost_rhs[...])
            rates[:, 0:HALF] += lifted[0:ROWS]
            rates[:, HALF:WIDE] += lifted[ROWS : 2 * ROWS]
        else:
            rates[:, 0:HALF] += dot(lift[0:ROWS, :], ghost_rhs[...])

    def inject(turn, moment):
        values = jnp.where(
            comp_id == 0,
            left[turn, moment, 0:1, :],
            jnp.where(comp_id == 1, left[turn, moment, 1:2, :], left[turn, moment, 2:3, :]),
        )
        high, low = split(pick_row[...] * values)
        return dot(jnp.concatenate([high, low], axis=1), pick_back[...])

    def gather(halves, turn, moment):
        both = dot(halves, pick_lane[...])
        chosen = (both[0:ROWS] + both[ROWS : 2 * ROWS]) * pick_row[...]
        out = jnp.zeros((8, 128), F32)
        for comp in range(3):
            part = jnp.sum(jnp.where(comp_id == comp, chosen, 0.0), axis=0, keepdims=True)
            out = jnp.where(sub8 == comp, part, out)
        left[turn, moment] = out

    def nothing():
        pass

    def to_output_order(vector, number):
        for moment in range(2):
            both = dot_nt(jnp.concatenate(split(vector[moment]), axis=0), order[...])
            at = (number * 2 + moment) * ROWS
            perm_out[at : at + ROWS, :] = both[0:ROWS] + both[ROWS : 2 * ROWS]

    every, electric = (0, 1), (0,)

    def sweep(turn, carry):
        fields[:, 0:HALF] = inject(turn, 1)
        fields[:, HALF:WIDE] = jnp.zeros((ROWS, HALF), F32)

        def second_1():
            second[...] = rates[...]

        def merge_1(lifted):
            second[:, 0:HALF] += lifted[0:ROWS]
            second[:, HALF:WIDE] += lifted[ROWS : 2 * ROWS]

        def late_1():
            @pl.when(turn == 1)
            def _():
                reduce_send(0, 1, reduce_take(0, 0))
                to_output_order(source.at[0], 0)

        stage(turn * 3, nothing, second_1, late_1, merge_1, every, every, False, 1.0)
        for k in range(5):
            source[turn, 1, :, lanes(k)] = gain[:, lanes(k)] * (fields[:, lanes(k)] + 0.5 * second[:, lanes(k)])
        fields[:, 0:HALF] = inject(turn, 0) + fields[:, 0:HALF] + second[:, 0:HALF] + 0.5 * rates[:, 0:HALF]
        fields[:, HALF:WIDE] = second[:, HALF:WIDE] + 0.5 * rates[:, HALF:WIDE]

        def second_2():
            for k in range(5):
                amount = gain[:, lanes(k)] * (fields[:, lanes(k)] + 0.5 * rates[:, lanes(k)])
                source[turn, 0, :, lanes(k)] = amount
                second[:, lanes(k)] = gain[:, lanes(k)] * amount
            second[:, HALF:WIDE] = jnp.zeros((ROWS, HALF), F32)

        def merge_2(lifted):
            for k in range(5):
                amount = source[turn, 0, :, lanes(k)] + 0.5 * gain[:, lanes(k)] * lifted[0:ROWS, lanes(k)]
                source[turn, 0, :, lanes(k)] = amount
                second[:, lanes(k)] = gain[:, lanes(k)] * amount

        def late_2():
            @pl.when(turn == 0)
            def _():
                for copy in support_copies:
                    copy.wait()
                for face in range(FACES):
                    for k in range(5):
                        column = float(root[k] ** 2) * cols_ref[face * 16 : face * 16 + 16, 5:6]
                        gain_out[face * 16 : face * 16 + 16, lanes(k)] = column * beside_support[face]

            @pl.when(turn == 1)
            def _():
                reduce_send(0, 2, reduce_take(0, 1))

        stage(turn * 3 + 1, nothing, second_2, late_2, merge_2, electric, every, True, 0.5)
        fields[:, 0:HALF] = second[:, 0:HALF] + 0.5 * rates[:, 0:HALF]
        fields[:, HALF:WIDE] = 0.5 * rates[:, HALF:WIDE]

        def early_3():
            gather(rhs[0:160, 0:HALF], turn + 1, 0)

        def second_3():
            for k in range(5):
                drive = gain[:, lanes(k)] * source[turn, 1, :, lanes(k)]
                second[:, lanes(k)] = fields[:, lanes(k)] + 0.5 * (rates[:, lanes(k)] + drive)
                fields[:, lanes(k)] = fields[:, lanes(k)] + drive
            second[:, HALF:WIDE] = fields[:, HALF:WIDE] + 0.5 * rates[:, HALF:WIDE]

        def merge_3(lifted):
            second[:, 0:HALF] += 0.5 * lifted[0:ROWS]
            second[:, HALF:WIDE] += 0.5 * lifted[ROWS : 2 * ROWS]

        def late_3():
            @pl.when(turn == 0)
            def _():
                reduce_send(
                    0, 0, packed_row([data_dot(left[0], left[0]), source_dot(source.at[0], source.at[0])])
                )

            @pl.when(turn == 1)
            def _():
                norms = reduce_take(0, 2)
                red_buf[0, 0, 0] = norms
                ratio = entry(norms, 1) / entry(norms, 0)
                for moment in range(2):
                    for k in range(5):
                        ortho[moment, :, lanes(k)] = (
                            source[1, moment, :, lanes(k)] - ratio * source[0, moment, :, lanes(k)]
                        )
                to_output_order(ortho, 1)

        stage(turn * 3 + 2, early_3, second_3, late_3, merge_3, every, electric, False, 0.5)
        halves = split(fields[:, 0:HALF] + rates[:, 0:HALF])
        gather(jnp.concatenate(halves, axis=0), turn + 1, 1)
        return carry

    lax.fori_loop(0, 2, sweep, 0)

    norms = red_buf[0, 0, 0]
    sq_b, sq_g = entry(norms, 0), entry(norms, 1)
    ratio = sq_g / sq_b
    for moment in range(2):
        left[0, moment] = left[1, moment] - ratio * left[0, moment]
        left[2, moment] = left[2, moment] - ratio * left[1, moment]
    p, f, h = left[0], left[1], left[2]
    products = [
        data_dot(p, p), source_dot(ortho, ortho), source_dot(ortho, source.at[0]), data_dot(h, h), data_dot(h, f),
        data_dot(f, f), data_dot(h, p), data_dot(f, p),
    ]
    reduce_send(1, 0, packed_row(products))
    reduce_send(1, 1, reduce_take(1, 0))
    reduce_send(1, 2, reduce_take(1, 1))
    total = reduce_take(1, 2)
    pp, oo, og, hh, hf, ff, hp, fp = (entry(total, number) for number in range(8))
    take = pp / sq_g
    sq_q = jnp.maximum(oo - 2.0 * take * og + take * take * sq_g, 0.0)
    beta_1 = jnp.sqrt(sq_b)
    alpha_1 = jnp.sqrt(ratio)
    beta_2 = jnp.sqrt(take)
    alpha_2 = jnp.sqrt(sq_q / pp)
    sq_w = hh - 2.0 * take * hf + take * take * ff
    sq_beta_3 = jnp.maximum(sq_w / sq_q - 2.0 * (hp - take * fp) / pp + sq_q / pp, 0.0)
    rho_1 = jnp.sqrt(alpha_1 * alpha_1 + beta_2 * beta_2)
    cosine, sine = alpha_1 / rho_1, beta_2 / rho_1
    step_1 = cosine * beta_1 / rho_1
    phi_bar = sine * beta_1
    theta = sine * alpha_2
    rho_bar = -cosine * alpha_2
    rho_2 = jnp.sqrt(rho_bar * rho_bar + sq_beta_3)
    step_2 = rho_bar / rho_2 * phi_bar / rho_2
    on_ortho = step_2 / jnp.sqrt(sq_q)
    on_first = (step_1 - step_2 * theta / rho_1) / jnp.sqrt(sq_g) - on_ortho * take
    on_h = phi_bar / rho_2 / jnp.sqrt(sq_q)
    on_p = phi_bar / rho_2 * jnp.sqrt(sq_q) / pp
    for moment in range(2):
        res_ref[moment] = (on_h * (h[moment] - take * f[moment]) - on_p * p[moment])[0:3, :]
        for comp in range(3):
            for i in range(5):
                at = comp * 25 + i * 5
                one = perm_out[moment * ROWS + at : moment * ROWS + at + 5, :]
                two = perm_out[(2 + moment) * ROWS + at : (2 + moment) * ROWS + at + 5, :]
                est_ref[moment, comp, i] = on_first * one + on_ortho * two


def solution(mesh):
    n_gx, n_gy = mesh.shape["gx"], mesh.shape["gy"]
    matrices, columns = tables()

    def shards(probe_data, conductivity, support, face_tags, probe_nodes):
        vmem = pl.BlockSpec(memory_space=pltpu.VMEM)
        smem = pl.BlockSpec(memory_space=pltpu.SMEM)
        anywhere = pl.BlockSpec(memory_space=pl.ANY)
        return pl.pallas_call(
            functools.partial(kernel, n_gx, n_gy),
            out_shape=(
                jax.ShapeDtypeStruct((2, 3, 5, 5, HALF), F32),
                jax.ShapeDtypeStruct((2, 3, 128), F32),
            ),
            in_specs=[smem] + [anywhere] * 6,
            out_specs=(vmem, vmem),
            scratch_shapes=[
                pltpu.VMEM((3, 2, 128), F32),
                pltpu.VMEM((5, 5, HALF), F32),
                pltpu.VMEM((1, 1, 128), jnp.int32),
                pltpu.VMEM((1, 128), jnp.int32),
                pltpu.VMEM(matrices.shape, F32),
                pltpu.VMEM(columns.shape, F32),
                pltpu.VMEM(matrices.shape, BF16),
                pltpu.VMEM((HALF, HALF), BF16),
                pltpu.VMEM((3, ROWS, 128), F32),
                pltpu.VMEM((ROWS, WIDE), F32),
                pltpu.VMEM((ROWS, WIDE), F32),
                pltpu.VMEM((ROWS, WIDE), F32),
                pltpu.VMEM((256, WIDE), BF16),
                pltpu.VMEM((INNER, WIDE), F32),
                pltpu.VMEM((128, HALF), BF16),
                pltpu.VMEM((64, HALF), BF16),
                pltpu.VMEM((ROWS, HALF), F32),
                pltpu.VMEM((ROWS, HALF), F32),
                pltpu.VMEM((64, HALF), F32),
                pltpu.VMEM((ROWS, 128), F32),
                pltpu.VMEM((HALF, 128), BF16),
                pltpu.VMEM((256, HALF), BF16),
                pltpu.VMEM((3, 2, 8, 128), F32),
                pltpu.VMEM((2, 2, ROWS, HALF), F32),
                pltpu.VMEM((2, ROWS, HALF), F32),
                pltpu.VMEM((ROWS, HALF), F32),
                pltpu.VMEM((4 * ROWS, HALF), F32),
                pltpu.VMEM((5, 1, 128), F32),
                pltpu.VMEM((6, FACES, QROWS, 128), F32),
                pltpu.VMEM((6, FACES, QROWS, 128), F32),
                pltpu.VMEM((6, FACES, QROWS, 128), F32),
                pltpu.VMEM((6, FACES, QROWS, 128), F32),
                pltpu.VMEM((6, 4, 24, 128), F32),
                pltpu.VMEM((6, 4, 24, 128), F32),
                pltpu.VMEM((2, 3, 8, 1, 128), F32),
                pltpu.SemaphoreType.DMA((6,)),
                pltpu.SemaphoreType.DMA((6, FACES)),
                pltpu.SemaphoreType.DMA((6, FACES)),
                pltpu.SemaphoreType.DMA((6, FACES)),
                pltpu.SemaphoreType.DMA((6, FACES)),
                pltpu.SemaphoreType.DMA((6, 4)),
                pltpu.SemaphoreType.DMA((6, 4)),
                pltpu.SemaphoreType.DMA((2, 3)),
                pltpu.SemaphoreType.DMA((2, 3)),
                pltpu.SemaphoreType.DMA((FACES,)),
                pltpu.SemaphoreType.DMA((FACES,)),
            ],
            compiler_params=pltpu.CompilerParams(
                collective_id=0, has_side_effects=True, vmem_limit_bytes=56 * 1024 * 1024
            ),
        )(
            jnp.transpose(face_tags, (1, 2, 0)), jnp.transpose(probe_data, (1, 0, 2)), conductivity, support,
            probe_nodes.reshape(1, 128), jnp.asarray(matrices), jnp.asarray(columns),
        )

    return jax.shard_map(
        shards,
        mesh=mesh,
        in_specs=(
            P(None, None, ("gx", "gy")),
            P("gx", "gy", None),
            P("gx", "gy", None),
            P(None, "gx", "gy"),
            P(("gx", "gy")),
        ),
        out_specs=(P(None, None, "gx", "gy", None), P(None, None, ("gx", "gy"))),
        check_vma=False,
    )
```

time: 99.4 us -> 69.7 us (0.70)
  Pallas kernels: 88.9 us -> 66 us
  local copies, waits for them, and re-layouts: 9.07 us -> 2.6 us
    pallas_call x1, Pallas kernels: 88.9 us -> 66 us  [shards(): pl.pallas_call(functools.partial(kernel, n_gx, n_gy), out_shape=(jax.Shap...]
    unnamed x24 -> x2, local copies, waits for them, and re-layouts: 7.55 us -> 0.01 us
    pallas_call x2, local copies, waits for them, and re-layouts: 1.52 us -> 2.59 us  [shards(): pl.pallas_call(functools.partial(kernel, n_gx, n_gy), out_shape=(jax.Shap...]
where the time goes in v2:
time: 69.7 us; the launch traced here: 69.2 us
  Pallas kernels  66 us (95%)
  local copies, waits for them, and re-layouts  2.6 us (4%)
    pallas_call x1, Pallas kernels, shards(): pl.pallas_call(functools.partial(kernel, n_gx, n_gy), out_shape=(jax.Shap...  66 us
    pallas_call x2, local copies, waits for them, and re-layouts, shards(): pl.pallas_call(functools.partial(kernel, n_gx, n_gy), out_shape=(jax.Shap...  2.59 us

profile of v2, /device:TPU:1, one launch (start us, length us, event | category | flops | bytes accessed | tf_op | source)
XLA Modules:
  0.0 69.2 jit_solution(12276743619594211267)
XLA Ops:
  0.6 66.0 %shard_map.86 = (f32[2,3,5,5,640]{4,3,2,1,0:T(8,128)}, f32[2,3,128]{2,1,0:T(4,128)}) custom-call(s32[1,1,2]{2,1,0:T(1,128)} %bitcast.4, f32[3,2,128]{2,1,0:T(2,128)} %bitcast.3, f32[5,5,640]{2,1,0:T(8,128)} %cond_hbm.1, s32[1,1,128]{2,1,0:T(1,128)} %supp_hbm.1, s32[1,128]{1,0:T(1,128)} %bitcast.5, f32[624,256]{1,0:T(8,128)} %constant.4.clone.mats_hbm, ...), custom_call_target="tpu_custom_call" | custom-call | tf_op jit(solution)/shard_map/pallas_call | solution.py:664
  66.6 0.0 copy-start
  66.6 2.0 %copy.9 = f32[2,3,5,5,640]{4,0,3,2,1:T(2,128)} copy(f32[2,3,5,5,640]{4,3,2,1,0:T(8,128)} %get-tuple-element.2) | data formatting | bytes 768000 | tf_op jit(solution)/shard_map/pallas_call | solution.py:664
  68.7 0.0 copy-done
  68.7 0.6 copy.10
Async XLA Ops:
  66.6 2.0 %copy-start = (f32[2,3,128]{2,1,0:T(4,128)S(1)}, f32[2,3,128]{2,1,0:T(4,128)}, u32[]{:S(2)}) copy-start(f32[2,3,128]{2,1,0:T(4,128)} %get-tuple-element.3) | copy-start | bytes 9220

commit v3 on v2

--- a/solution.py
+++ b/solution.py
@@ -16,8 +16,6 @@
 STEP_SIZE = 0.02
 LIFT_HALF = 5.0
 DRIVE_GAIN = 50.0
-NX_CHIPS = 4
-CORES = 2
 ROWS = 80
 QROWS = 56
 HALF = 640
@@ -164,8 +162,8 @@
 
 
 def kernel(
-    n_gx, n_gy, tags_ref, data_hbm, cond_hbm, supp_hbm, nodes_hbm, mats_hbm, cols_hbm, est_ref, res_ref,
-    data_ref, cond_ref, supp_ref, nodes_ref, mats_ref, cols_ref, mats, order, spread,
+    n_gx, n_gy, tags_hbm, data_hbm, cond_hbm, supp_hbm, nodes_hbm, mats_hbm, cols_hbm, est_ref, res_ref,
+    tags_ref, data_ref, cond_ref, supp_ref, nodes_ref, mats_ref, cols_ref, mats, order, spread,
     fields, second, rates, rhs, prod, ghost_rhs, corner_rhs, sig, gain, gain_out, pick_row, pick_lane, pick_back,
     left, source, ortho, perm, perm_out, beside_support,
     send_buf, recv_buf, send_next, recv_next, send_diag, recv_diag, red_buf,
@@ -175,7 +173,7 @@
     loads = []
     pairs = (
         (data_hbm, data_ref), (nodes_hbm, nodes_ref), (mats_hbm, mats_ref), (cols_hbm, cols_ref),
-        (cond_hbm, cond_ref), (supp_hbm, supp_ref),
+        (cond_hbm, cond_ref), (supp_hbm, supp_ref), (tags_hbm, tags_ref),
     )
     for number, (far, near) in enumerate(pairs):
         load = pltpu.make_async_copy(far, near, load_sem.at[number])
@@ -185,18 +183,12 @@
     deriv, root = lobatto_scaled()
     deriv = STEP_SIZE * deriv
     gx, gy = lax.axis_index("gx"), lax.axis_index("gy")
-    x_at, z_at = lax.rem(gx, NX_CHIPS), lax.div(gx, NX_CHIPS)
-    core_at, y_at = lax.rem(gy, CORES), lax.div(gy, CORES)
-    n_z, n_y, n_xc = n_gx // NX_CHIPS, n_gy // CORES, NX_CHIPS * CORES
-    sizes = (n_xc, n_z, n_y)
+    sizes = (n_gx, n_gy)
 
     def partner(phase, step):
         if phase == 0:
-            spot = lax.rem(x_at * CORES + core_at + step, n_xc)
-            return (z_at * NX_CHIPS + lax.div(spot, CORES), y_at * CORES + lax.rem(spot, CORES))
-        if phase == 1:
-            return (lax.rem(z_at + step, n_z) * NX_CHIPS + x_at, gy)
-        return (gx, lax.rem(y_at + step, n_y) * CORES + core_at)
+            return (lax.rem(gx + step, n_gx), gy)
+        return (gx, lax.rem(gy + step, n_gy))
 
     def near_by(step_x, step_y):
         return (lax.rem(gx + n_gx + step_x, n_gx), lax.rem(gy + n_gy + step_y, n_gy))
@@ -214,10 +206,10 @@
 
     barrier = pltpu.get_barrier_semaphore()
     greeted = 0
-    for device in beside + across:
+    for device in across:
         pl.semaphore_signal(barrier, inc=1, device_id=device, device_id_type=MESH)
         greeted += 1
-    for phase in range(3):
+    for phase in range(2):
         for step in range(1, sizes[phase]):
             pl.semaphore_signal(barrier, inc=1, device_id=partner(phase, step), device_id_type=MESH)
             greeted += 1
@@ -273,8 +265,8 @@
         for moment in range(2):
             left[0, moment, comp : comp + 1, :] = data_ref[comp, moment : moment + 1, :]
 
-    tag_low = tags_ref[0, 0, 0].astype(F32)
-    tag_high = tags_ref[0, 0, 1].astype(F32)
+    tag_low = tags_ref[0][:, 0:1].astype(F32)
+    tag_high = tags_ref[0][:, 1:2].astype(F32)
     for comp in range(3):
         for i in range(5):
             perm[comp * 25 + i * 5 : comp * 25 + i * 5 + 5, :] = cond_ref[i]
@@ -309,10 +301,10 @@
         others = red_buf.at[index, phase, pl.ds(1, sizes[phase] - 1)]
         pltpu.make_async_copy(others, others, red_recv_sem.at[index, phase]).wait()
         pltpu.make_async_copy(others, others, red_send_sem.at[index, phase]).wait()
-        total = red_buf[index, phase, 0]
-        for step in range(1, sizes[phase]):
-            total = total + red_buf[index, phase, step]
-        return total
+        terms = [red_buf[index, phase, step] for step in range(sizes[phase])]
+        while len(terms) > 1:
+            terms = [sum(terms[at + 1 : at + 2], terms[at]) for at in range(0, len(terms), 2)]
+        return terms[0]
 
     def whole(value):
         return jnp.sum(jnp.sum(value, axis=0, keepdims=True), axis=1, keepdims=True)
@@ -336,22 +328,38 @@
                 total = total + a[moment, :, lanes(k)] * b[moment, :, lanes(k)]
         return whole(total)
 
-    def load_rhs(ref, blocks=10):
-        for block in range(blocks):
+    def load_rhs(ref, magnetic):
+        for block in range(10 if magnetic else 5):
             high, low = split(ref[:, lanes(block)])
             rhs[0:80, lanes(block)] = high
             rhs[80:160, lanes(block)] = low
             rhs[160:240, lanes(block)] = high
 
-    def own_rates(field, result, halves):
-        if len(halves) == 2:
+    def own_rates(field, result, halves, magnetic):
+        if not magnetic:
+            prod[:, 0:HALF] = dot(inner[...], rhs[:, 0:HALF])
+        elif len(halves) == 1:
+            prod[:, HALF:WIDE] = dot(inner[...], rhs[:, HALF:WIDE])
+        else:
             prod[...] = dot(inner[...], rhs[...])
-        else:
-            prod[:, HALF:WIDE] = dot(inner[...], rhs[:, HALF:WIDE])
         for half in halves:
             own0, other0 = half * 5, (1 - half) * 5
             sign = 1.0 if half == 0 else -1.0
             for k in range(5):
+                if half == 0 and not magnetic:
+                    change = -sig[:, lanes(k)] * field[:, lanes(k)]
+                    upper = change[0:QROWS]
+                    if k == 0:
+                        inward = pltpu.roll(field[0:QROWS, lanes(4)], 1, 1)
+                        edge = -tag_low * field[0:QROWS, lanes(0)]
+                        upper = upper + spread[2][0:QROWS] * jnp.where(lane56 == 0, edge, inward)
+                    elif k == 4:
+                        inward = pltpu.roll(field[0:QROWS, lanes(0)], 127, 1)
+                        edge = -tag_high * field[0:QROWS, lanes(4)]
+                        upper = upper + spread[2][0:QROWS] * jnp.where(lane56 == 127, edge, inward)
+                    result[0:QROWS, lanes(k)] = upper
+                    result[QROWS:ROWS, lanes(k)] = change[QROWS:ROWS]
+                    continue
                 slope = None
                 for m in range(5):
                     if m != k and abs(deriv[k, m]) > 1e-12:
@@ -400,9 +408,11 @@
         ghost_rhs[face * 16 : face * 16 + 16, lanes(k)] = high
         ghost_rhs[64 + face * 16 : 64 + face * 16 + 16, lanes(k)] = low
 
-    def stage(slot, early, make_second, late, merge, halves_1, halves_2, masked, share):
-        load_rhs(fields)
-        out = dot(send_e[...], rhs[:, 0:HALF]) + dot(send_h[...], rhs[:, HALF:WIDE])
+    def stage(slot, early, make_second, late, merge, halves_1, halves_2, magnetic_1, magnetic_2, share):
+        load_rhs(fields, magnetic_1)
+        out = dot(send_e[...], rhs[:, 0:HALF])
+        if magnetic_1:
+            out = out + dot(send_h[...], rhs[:, HALF:WIDE])
         copies = []
         for face in range(FACES):
             pack_face(out, face, send_buf.at[slot, face])
@@ -427,11 +437,11 @@
                 )
             )
         early()
-        own_rates(fields, rates, halves_1)
+        own_rates(fields, rates, halves_1, magnetic_1)
         make_second()
-        load_rhs(second)
+        load_rhs(second, magnetic_2)
         out = dot(send_e[0:64, :], rhs[:, 0:HALF])
-        if not masked:
+        if magnetic_2:
             out = out + dot(send_h[0:64, :], rhs[:, HALF:WIDE])
         next_copies = []
         for face in range(FACES):
@@ -450,8 +460,8 @@
             for k in range(5):
                 set_ghosts(face, k, unpack_face(recv_buf.at[slot, face], k))
         merge(dot(lift[...], ghost_rhs[...]))
-        load_rhs(second)
-        own_rates(second, rates, halves_2)
+        load_rhs(second, magnetic_2)
+        own_rates(second, rates, halves_2, magnetic_2)
 
         for copy in corner_copies:
             copy.wait()
@@ -465,7 +475,7 @@
                 high, low = split(jnp.concatenate(pieces, axis=0))
                 corner_rhs[16 * two : 16 * two + 16, lanes(k)] = high
                 corner_rhs[32 + 16 * two : 32 + 16 * two + 16, lanes(k)] = low
-        start = at_corner + (64 if masked else 0)
+        start = at_corner + (0 if magnetic_2 else 64)
         extra = dot(mats[start : start + 64, 0:64], corner_rhs[...])
         for copy in next_copies:
             copy.wait()
@@ -473,7 +483,7 @@
             for k in range(5):
                 piece = extra[face * 16 : face * 16 + 16, lanes(k)]
                 piece = jnp.concatenate([piece[0:8], jnp.where(kept(k), piece[8:16], 0.0)], axis=0)
-                if masked:
+                if not magnetic_2:
                     piece = piece + strength * unpack_face(send_buf.at[slot, face ^ 1], k)
                     piece = piece * gain_out[face * 16 : face * 16 + 16, lanes(k)]
                 set_ghosts(face, k, unpack_face(recv_next.at[slot, face], k) + share * piece)
@@ -530,7 +540,7 @@
                 reduce_send(0, 1, reduce_take(0, 0))
                 to_output_order(source.at[0], 0)
 
-        stage(turn * 3, nothing, second_1, late_1, merge_1, every, every, False, 1.0)
+        stage(turn * 3, nothing, second_1, late_1, merge_1, every, every, False, True, 1.0)
         for k in range(5):
             source[turn, 1, :, lanes(k)] = gain[:, lanes(k)] * (fields[:, lanes(k)] + 0.5 * second[:, lanes(k)])
         fields[:, 0:HALF] = inject(turn, 0) + fields[:, 0:HALF] + second[:, 0:HALF] + 0.5 * rates[:, 0:HALF]
@@ -559,11 +569,7 @@
                         column = float(root[k] ** 2) * cols_ref[face * 16 : face * 16 + 16, 5:6]
                         gain_out[face * 16 : face * 16 + 16, lanes(k)] = column * beside_support[face]
 
-            @pl.when(turn == 1)
-            def _():
-                reduce_send(0, 2, reduce_take(0, 1))
-
-        stage(turn * 3 + 1, nothing, second_2, late_2, merge_2, electric, every, True, 0.5)
+        stage(turn * 3 + 1, nothing, second_2, late_2, merge_2, electric, every, True, False, 0.5)
         fields[:, 0:HALF] = second[:, 0:HALF] + 0.5 * rates[:, 0:HALF]
         fields[:, HALF:WIDE] = 0.5 * rates[:, HALF:WIDE]
 
@@ -590,7 +596,7 @@
 
             @pl.when(turn == 1)
             def _():
-                norms = reduce_take(0, 2)
+                norms = reduce_take(0, 1)
                 red_buf[0, 0, 0] = norms
                 ratio = entry(norms, 1) / entry(norms, 0)
                 for moment in range(2):
@@ -600,7 +606,7 @@
                         )
                 to_output_order(ortho, 1)
 
-        stage(turn * 3 + 2, early_3, second_3, late_3, merge_3, every, electric, False, 0.5)
+        stage(turn * 3 + 2, early_3, second_3, late_3, merge_3, every, electric, True, True, 0.5)
         halves = split(fields[:, 0:HALF] + rates[:, 0:HALF])
         gather(jnp.concatenate(halves, axis=0), turn + 1, 1)
         return carry
@@ -620,8 +626,7 @@
     ]
     reduce_send(1, 0, packed_row(products))
     reduce_send(1, 1, reduce_take(1, 0))
-    reduce_send(1, 2, reduce_take(1, 1))
-    total = reduce_take(1, 2)
+    total = reduce_take(1, 1)
     pp, oo, og, hh, hf, ff, hp, fp = (entry(total, number) for number in range(8))
     take = pp / sq_g
     sq_q = jnp.maximum(oo - 2.0 * take * og + take * take * sq_g, 0.0)
@@ -659,7 +664,6 @@
 
     def shards(probe_data, conductivity, support, face_tags, probe_nodes):
         vmem = pl.BlockSpec(memory_space=pltpu.VMEM)
-        smem = pl.BlockSpec(memory_space=pltpu.SMEM)
         anywhere = pl.BlockSpec(memory_space=pl.ANY)
         return pl.pallas_call(
             functools.partial(kernel, n_gx, n_gy),
@@ -667,9 +671,10 @@
                 jax.ShapeDtypeStruct((2, 3, 5, 5, HALF), F32),
                 jax.ShapeDtypeStruct((2, 3, 128), F32),
             ),
-            in_specs=[smem] + [anywhere] * 6,
+            in_specs=[anywhere] * 7,
             out_specs=(vmem, vmem),
             scratch_shapes=[
+                pltpu.VMEM((1, 1, 2), jnp.int32),
                 pltpu.VMEM((3, 2, 128), F32),
                 pltpu.VMEM((5, 5, HALF), F32),
                 pltpu.VMEM((1, 1, 128), jnp.int32),
@@ -704,21 +709,21 @@
                 pltpu.VMEM((6, FACES, QROWS, 128), F32),
                 pltpu.VMEM((6, 4, 24, 128), F32),
                 pltpu.VMEM((6, 4, 24, 128), F32),
-                pltpu.VMEM((2, 3, 8, 1, 128), F32),
-                pltpu.SemaphoreType.DMA((6,)),
+                pltpu.VMEM((2, 2, max(n_gx, n_gy), 1, 128), F32),
+                pltpu.SemaphoreType.DMA((7,)),
                 pltpu.SemaphoreType.DMA((6, FACES)),
                 pltpu.SemaphoreType.DMA((6, FACES)),
                 pltpu.SemaphoreType.DMA((6, FACES)),
                 pltpu.SemaphoreType.DMA((6, FACES)),
                 pltpu.SemaphoreType.DMA((6, 4)),
                 pltpu.SemaphoreType.DMA((6, 4)),
-                pltpu.SemaphoreType.DMA((2, 3)),
-                pltpu.SemaphoreType.DMA((2, 3)),
+                pltpu.SemaphoreType.DMA((2, 2)),
+                pltpu.SemaphoreType.DMA((2, 2)),
                 pltpu.SemaphoreType.DMA((FACES,)),
                 pltpu.SemaphoreType.DMA((FACES,)),
             ],
             compiler_params=pltpu.CompilerParams(
-                collective_id=0, has_side_effects=True, vmem_limit_bytes=56 * 1024 * 1024
+                collective_id=0, has_side_effects=True, vmem_limit_bytes=22 * 1024 * 1024
             ),
         )(
             jnp.transpose(face_tags, (1, 2, 0)), jnp.transpose(probe_data, (1, 0, 2)), conductivity, support,

time: 69.7 us -> 71.4 us (1.024)
  local copies, waits for them, and re-layouts: 2.6 us -> 4.94 us
    unnamed x2 -> x14, local copies, waits for them, and re-layouts: 0.01 us -> 3.42 us
    pallas_call x2, local copies, waits for them, and re-layouts: 2.59 us -> 1.52 us  [shards(): pl.pallas_call(functools.partial(kernel, n_gx, n_gy), out_shape=(jax.Shap...]
where the time goes in v3:
time: 71.4 us; the launch traced here: 71.1 us
  Pallas kernels  65.5 us (92%)
  local copies, waits for them, and re-layouts  4.94 us (7%)
    pallas_call x1, Pallas kernels, shards(): pl.pallas_call(functools.partial(kernel, n_gx, n_gy), out_shape=(jax.Shap...  65.5 us
    unnamed x14, local copies, waits for them, and re-layouts  3.42 us
    pallas_call x2, local copies, waits for them, and re-layouts, shards(): pl.pallas_call(functools.partial(kernel, n_gx, n_gy), out_shape=(jax.Shap...  1.52 us

profile of v3, /device:TPU:1, one launch (start us, length us, event | category | flops | bytes accessed | tf_op | source)
XLA Modules:
  0.0 71.1 jit_solution(15512534205059365360)
XLA Ops:
  0.6 0.0 copy-start.3
  0.6 0.0 copy-start.4
  0.7 0.0 copy-start.5
  0.7 0.0 copy-start.6
  0.7 0.6 copy-done.3
  1.3 0.0 copy-done.4
  1.3 0.0 copy-done.5
  1.3 0.0 copy-done.6
  1.3 0.0 copy-start
  1.3 1.1 %copy-done = f32[624,256]{1,0:T(8,128)S(1)} copy-done((f32[624,256]{1,0:T(8,128)S(1)}, f32[624,256]{1,0:T(8,128)}, u32[]{:S(2)}) %copy-start) | copy-done | bytes 639000
  2.4 0.0 copy-start.1
  2.4 0.9 %copy-done.1 = f32[5,5,640]{2,1,0:T(8,128)S(1)} copy-done((f32[5,5,640]{2,1,0:T(8,128)S(1)}, f32[5,5,640]{2,1,0:T(8,128)}, u32[]{:S(2)}) %copy-start.1) | copy-done | bytes 64024
  3.3 0.0 copy-start.2
  3.3 0.8 %copy-done.2 = f32[80,128]{1,0:T(8,128)S(1)} copy-done((f32[80,128]{1,0:T(8,128)S(1)}, f32[80,128]{1,0:T(8,128)}, u32[]{:S(2)}) %copy-start.2) | copy-done | bytes 40984
  4.1 65.5 %shard_map.86 = (f32[2,3,5,5,640]{4,3,2,1,0:T(8,128)S(1)}, f32[2,3,128]{2,1,0:T(4,128)S(1)}) custom-call(s32[1,1,2]{2,1,0:T(1,128)S(1)} %bitcast.4, f32[3,2,128]{2,1,0:T(2,128)S(1)} %bitcast.3, f32[5,5,640]{2,1,0:T(8,128)S(1)} %copy-done.1, s32[1,1,128]{2,1,0:T(1,128)S(1)} %copy-done.5, s32[1,128]{1,0:T(1,128)S(1)} %bitcast.5, f32[624,256]{1,0:T(8,128)S(1)} %copy-done, ...), custom_call_target="tpu_custom_call" | custom-call | tf_op jit(solution)/shard_map/pallas_call | solution.py:668
  69.6 0.9 %copy.9 = f32[2,3,5,5,640]{4,0,3,2,1:T(2,128)} copy(f32[2,3,5,5,640]{4,3,2,1,0:T(8,128)S(1)} %get-tuple-element.2) | data formatting | bytes 768000 | tf_op jit(solution)/shard_map/pallas_call | solution.py:668
  70.5 0.6 copy.10
Async XLA Ops:
  0.6 0.7 copy-start.3
  0.6 0.7 copy-start.4
  0.7 0.7 copy-start.5
  0.7 0.7 copy-start.6
  1.3 1.1 %copy-start = (f32[624,256]{1,0:T(8,128)S(1)}, f32[624,256]{1,0:T(8,128)}, u32[]{:S(2)}) copy-start(f32[624,256]{1,0:T(8,128)} %constant.4.clone.mats_hbm) | copy-start | bytes 1916932
  2.4 0.9 %copy-start.1 = (f32[5,5,640]{2,1,0:T(8,128)S(1)}, f32[5,5,640]{2,1,0:T(8,128)}, u32[]{:S(2)}) copy-start(f32[5,5,640]{2,1,0:T(8,128)} %cond_hbm.1) | copy-start | bytes 192004
  3.3 0.8 %copy-start.2 = (f32[80,128]{1,0:T(8,128)S(1)}, f32[80,128]{1,0:T(8,128)}, u32[]{:S(2)}) copy-start(f32[80,128]{1,0:T(8,128)} %constant.5.clone.cols_hbm) | copy-start | bytes 122884

commit v4 on v3

--- a/solution.py
+++ b/solution.py
@@ -726,8 +726,13 @@
                 collective_id=0, has_side_effects=True, vmem_limit_bytes=22 * 1024 * 1024
             ),
         )(
-            jnp.transpose(face_tags, (1, 2, 0)), jnp.transpose(probe_data, (1, 0, 2)), conductivity, support,
-            probe_nodes.reshape(1, 128), jnp.asarray(matrices), jnp.asarray(columns),
+            *(
+                pltpu.with_memory_space_constraint(array, pltpu.HBM)
+                for array in (
+                    jnp.transpose(face_tags, (1, 2, 0)), jnp.transpose(probe_data, (1, 0, 2)), conductivity, support,
+                    probe_nodes.reshape(1, 128), jnp.asarray(matrices), jnp.asarray(columns),
+                )
+            )
         )
 
     return jax.shard_map(

time: 71.4 us -> 67.4 us (0.944)
  local copies, waits for them, and re-layouts: 4.94 us -> 1.52 us
    unnamed x14 -> x0, local copies, waits for them, and re-layouts: 3.42 us -> none
where the time goes in v4:
time: 67.4 us; the launch traced here: 67.3 us
  Pallas kernels  65.1 us (97%)
  local copies, waits for them, and re-layouts  1.52 us (2%)
    pallas_call x1, Pallas kernels, shards(): pl.pallas_call(functools.partial(kernel, n_gx, n_gy), out_shape=(jax.Shap...  65.1 us
    pallas_call x2, local copies, waits for them, and re-layouts, shards(): pl.pallas_call(functools.partial(kernel, n_gx, n_gy), out_shape=(jax.Shap...  1.52 us

profile of v4, /device:TPU:1, one launch (start us, length us, event | category | flops | bytes accessed | tf_op | source)
XLA Modules:
  0.0 67.3 jit_solution(7828237312805830356)
XLA Ops:
  0.6 65.1 %shard_map.86 = (f32[2,3,5,5,640]{4,3,2,1,0:T(8,128)S(1)}, f32[2,3,128]{2,1,0:T(4,128)S(1)}) custom-call(s32[1,1,2]{2,1,0:T(1,128)} %bitcast.4, f32[3,2,128]{2,1,0:T(2,128)} %bitcast.3, f32[5,5,640]{2,1,0:T(8,128)} %cond_hbm.1, s32[1,1,128]{2,1,0:T(1,128)} %supp_hbm.1, s32[1,128]{1,0:T(1,128)} %bitcast.5, f32[624,256]{1,0:T(8,128)} %constant.4.clone.mats_hbm, ...), custom_call_target="tpu_custom_call" | custom-call | tf_op jit(solution)/shard_map/pallas_call | solution.py:668
  65.8 0.9 %copy.9 = f32[2,3,5,5,640]{4,0,3,2,1:T(2,128)} copy(f32[2,3,5,5,640]{4,3,2,1,0:T(8,128)S(1)} %get-tuple-element.2) | data formatting | bytes 768000 | tf_op jit(solution)/shard_map/pallas_call | solution.py:668
  66.7 0.6 copy.10

commit v5 on v4

--- a/solution.py
+++ b/solution.py
@@ -165,10 +165,10 @@
     n_gx, n_gy, tags_hbm, data_hbm, cond_hbm, supp_hbm, nodes_hbm, mats_hbm, cols_hbm, est_ref, res_ref,
     tags_ref, data_ref, cond_ref, supp_ref, nodes_ref, mats_ref, cols_ref, mats, order, spread,
     fields, second, rates, rhs, prod, ghost_rhs, corner_rhs, sig, gain, gain_out, pick_row, pick_lane, pick_back,
-    left, source, ortho, perm, perm_out, beside_support,
+    left, source, ortho, perm, perm_out, beside_support, own_support,
     send_buf, recv_buf, send_next, recv_next, send_diag, recv_diag, red_buf,
     load_sem, send_sem, recv_sem, next_send_sem, next_recv_sem, diag_send_sem, diag_recv_sem, red_send_sem, red_recv_sem,
-    supp_send_sem, supp_recv_sem,
+    supp_send_sem, supp_recv_sem, meet_sem,
 ):
     loads = []
     pairs = (
@@ -197,29 +197,54 @@
     across = tuple(near_by(-side_x, -side_y) for side_x, side_y in DIAGS)
     strength = STEP_SIZE * LIFT_HALF
     has = {(0, -1): gx > 0, (0, 1): gx < n_gx - 1, (1, -1): gy > 0, (1, 1): gy < n_gy - 1}
-    open_faces = tuple(
-        jnp.where(has[key], strength, 0.0).astype(F32) for key in ((0, -1), (0, 1), (1, -1), (1, 1))
-    )
-    open_diags = tuple(
-        jnp.where(has[(0, side_x)] & has[(1, side_y)], strength, 0.0).astype(F32) for side_x, side_y in DIAGS
-    )
+    to_face = tuple(has[key] for key in ((0, 1), (0, -1), (1, 1), (1, -1)))
+    to_diag = tuple(has[(0, -side_x)] & has[(1, -side_y)] for side_x, side_y in DIAGS)
+
+    for face in range(FACES):
+
+        @pl.when(jnp.logical_not(to_face[face ^ 1]))
+        def _():
+            for slot in range(6):
+                recv_buf[slot, face] = jnp.zeros((QROWS, 128), F32)
+                recv_next[slot, face] = jnp.zeros((QROWS, 128), F32)
+            beside_support[face] = jnp.zeros((1, 128), F32)
+
+    for diag in range(4):
+
+        @pl.when(jnp.logical_not(to_diag[3 - diag]))
+        def _():
+            for slot in range(6):
+                recv_diag[slot, diag] = jnp.zeros((24, 128), F32)
 
     barrier = pltpu.get_barrier_semaphore()
-    greeted = 0
-    for device in across:
-        pl.semaphore_signal(barrier, inc=1, device_id=device, device_id_type=MESH)
-        greeted += 1
-    for phase in range(2):
-        for step in range(1, sizes[phase]):
-            pl.semaphore_signal(barrier, inc=1, device_id=partner(phase, step), device_id_type=MESH)
-            greeted += 1
+    greeted = jnp.int32(0)
+    for device, exists in zip(beside + across, to_face + to_diag):
+
+        @pl.when(exists)
+        def _():
+            pl.semaphore_signal(barrier, inc=1, device_id=device, device_id_type=MESH)
+
+        greeted = greeted + exists.astype(jnp.int32)
 
     def remote(src, dst, sem_out, sem_in, device):
         copy = pltpu.make_async_remote_copy(
             src_ref=src, dst_ref=dst, send_sem=sem_out, recv_sem=sem_in, device_id=device, device_id_type=MESH
         )
-        copy.start()
         return copy
+
+    def start(copy, exists):
+        @pl.when(exists)
+        def _():
+            copy.start()
+
+    def wait_all(copies, exist, flip):
+        for number, exists in enumerate(exist):
+            back = number ^ flip
+
+            @pl.when(exists)
+            def _():
+                copies[number].wait_send()
+                copies[back].wait_recv()
 
     z_id = lax.broadcasted_iota(jnp.int32, (HALF, 128), 0)
     five = 5 * lax.broadcasted_iota(jnp.int32, (HALF, 128), 1)
@@ -277,15 +302,43 @@
     support = supp_ref[0].astype(F32)
     for k in range(5):
         gain[:, lanes(k)] = (-DRIVE_GAIN * STEP_SIZE * float(root[k])) * support * cols_ref[:, 0:1]
-    beside_support[4] = support
+    own_support[...] = support
 
     pl.semaphore_wait(barrier, greeted)
     support_copies = [
         remote(
-            beside_support.at[4], beside_support.at[face], supp_send_sem.at[face], supp_recv_sem.at[face], beside[face]
+            own_support, beside_support.at[face], supp_send_sem.at[face], supp_recv_sem.at[face], beside[face]
         )
         for face in range(FACES)
     ]
+    for copy, exists in zip(support_copies, to_face):
+        start(copy, exists)
+
+    rounds = 0
+    while 2**rounds < max(n_gx, n_gy):
+        rounds += 1
+
+    def meet(turn, when, taken, sent):
+        def beyond(number):
+            for at, size, along_x in ((gx, n_gx, True), (gy, n_gy, False)):
+                distance = 2**number
+                if distance < size:
+                    yield at >= distance, ((gx - distance, gy) if along_x else (gx, gy - distance))
+                    yield at < size - distance, ((gx + distance, gy) if along_x else (gx, gy + distance))
+
+        @pl.when(turn == when)
+        def _():
+            if 0 <= taken < rounds:
+                count = jnp.int32(0)
+                for exists, _ in beyond(taken):
+                    count = count + exists.astype(jnp.int32)
+                pl.semaphore_wait(meet_sem.at[taken], count)
+            if sent < rounds:
+                for exists, device in beyond(sent):
+
+                    @pl.when(exists)
+                    def _():
+                        pl.semaphore_signal(meet_sem.at[sent], inc=1, device_id=device, device_id_type=MESH)
 
     def reduce_send(index, phase, row):
         red_buf[index, phase, 0] = row
@@ -293,7 +346,7 @@
             remote(
                 red_buf.at[index, phase, 0], red_buf.at[index, phase, step], red_send_sem.at[index, phase],
                 red_recv_sem.at[index, phase], partner(phase, step),
-            )
+            ).start()
 
     def reduce_take(index, phase):
         if sizes[phase] == 1:
@@ -404,7 +457,7 @@
         return jnp.concatenate([buf[8 * k : 8 * k + 8, :], jnp.where(kept(k), mixed, 0.0)], axis=0)
 
     def set_ghosts(face, k, piece):
-        high, low = split(open_faces[face] * piece)
+        high, low = split(strength * piece)
         ghost_rhs[face * 16 : face * 16 + 16, lanes(k)] = high
         ghost_rhs[64 + face * 16 : 64 + face * 16 + 16, lanes(k)] = low
 
@@ -422,6 +475,7 @@
                     beside[face],
                 )
             )
+            start(copies[face], to_face[face])
         corner_copies = []
         for diag in range(4):
             base = 64 + diag * 8
@@ -436,6 +490,7 @@
                     diag_recv_sem.at[slot, diag], across[diag],
                 )
             )
+            start(corner_copies[diag], to_diag[diag])
         early()
         own_rates(fields, rates, halves_1, magnetic_1)
         make_second()
@@ -452,10 +507,10 @@
                     next_recv_sem.at[slot, face], beside[face],
                 )
             )
+            start(next_copies[face], to_face[face])
         late()
 
-        for copy in copies:
-            copy.wait()
+        wait_all(copies, to_face, 1)
         for face in range(FACES):
             for k in range(5):
                 set_ghosts(face, k, unpack_face(recv_buf.at[slot, face], k))
@@ -463,22 +518,20 @@
         load_rhs(second, magnetic_2)
         own_rates(second, rates, halves_2, magnetic_2)
 
-        for copy in corner_copies:
-            copy.wait()
+        wait_all(corner_copies, to_diag, 3)
         for two in range(2):
             for k in range(5):
                 pieces = []
                 for diag in (2 * two, 2 * two + 1):
                     tile = recv_diag[slot, diag, 8 * (k // 2) : 8 * (k // 2) + 8, :]
                     tile = jnp.where(sub8 >= 4 if k % 2 else sub8 < 4, tile, 0.0)
-                    pieces.append(open_diags[diag] * tile)
+                    pieces.append(strength * tile)
                 high, low = split(jnp.concatenate(pieces, axis=0))
                 corner_rhs[16 * two : 16 * two + 16, lanes(k)] = high
                 corner_rhs[32 + 16 * two : 32 + 16 * two + 16, lanes(k)] = low
-        start = at_corner + (0 if magnetic_2 else 64)
-        extra = dot(mats[start : start + 64, 0:64], corner_rhs[...])
-        for copy in next_copies:
-            copy.wait()
+        begin = at_corner + (0 if magnetic_2 else 64)
+        extra = dot(mats[begin : begin + 64, 0:64], corner_rhs[...])
+        wait_all(next_copies, to_face, 1)
         for face in range(FACES):
             for k in range(5):
                 piece = extra[face * 16 : face * 16 + 16, lanes(k)]
@@ -512,9 +565,6 @@
             out = jnp.where(sub8 == comp, part, out)
         left[turn, moment] = out
 
-    def nothing():
-        pass
-
     def to_output_order(vector, number):
         for moment in range(2):
             both = dot_nt(jnp.concatenate(split(vector[moment]), axis=0), order[...])
@@ -535,12 +585,16 @@
             second[:, HALF:WIDE] += lifted[ROWS : 2 * ROWS]
 
         def late_1():
+            meet(turn, 0, -1, 0)
+
             @pl.when(turn == 1)
             def _():
-                reduce_send(0, 1, reduce_take(0, 0))
+                reduce_send(
+                    0, 0, packed_row([data_dot(left[0], left[0]), source_dot(source.at[0], source.at[0])])
+                )
                 to_output_order(source.at[0], 0)
 
-        stage(turn * 3, nothing, second_1, late_1, merge_1, every, every, False, True, 1.0)
+        stage(turn * 3, lambda: meet(turn, 1, 4, 5), second_1, late_1, merge_1, every, every, False, True, 1.0)
         for k in range(5):
             source[turn, 1, :, lanes(k)] = gain[:, lanes(k)] * (fields[:, lanes(k)] + 0.5 * second[:, lanes(k)])
         fields[:, 0:HALF] = inject(turn, 0) + fields[:, 0:HALF] + second[:, 0:HALF] + 0.5 * rates[:, 0:HALF]
@@ -560,21 +614,27 @@
                 second[:, lanes(k)] = gain[:, lanes(k)] * amount
 
         def late_2():
+            meet(turn, 0, 1, 2)
+
+            @pl.when(turn == 1)
+            def _():
+                reduce_send(0, 1, reduce_take(0, 0))
+
             @pl.when(turn == 0)
             def _():
-                for copy in support_copies:
-                    copy.wait()
+                wait_all(support_copies, to_face, 1)
                 for face in range(FACES):
                     for k in range(5):
                         column = float(root[k] ** 2) * cols_ref[face * 16 : face * 16 + 16, 5:6]
                         gain_out[face * 16 : face * 16 + 16, lanes(k)] = column * beside_support[face]
 
-        stage(turn * 3 + 1, nothing, second_2, late_2, merge_2, electric, every, True, False, 0.5)
+        stage(turn * 3 + 1, lambda: meet(turn, 0, 0, 1), second_2, late_2, merge_2, electric, every, True, False, 0.5)
         fields[:, 0:HALF] = second[:, 0:HALF] + 0.5 * rates[:, 0:HALF]
         fields[:, HALF:WIDE] = 0.5 * rates[:, HALF:WIDE]
 
         def early_3():
             gather(rhs[0:160, 0:HALF], turn + 1, 0)
+            meet(turn, 0, 2, 3)
 
         def second_3():
             for k in range(5):
@@ -588,11 +648,7 @@
             second[:, HALF:WIDE] += 0.5 * lifted[ROWS : 2 * ROWS]
 
         def late_3():
-            @pl.when(turn == 0)
-            def _():
-                reduce_send(
-                    0, 0, packed_row([data_dot(left[0], left[0]), source_dot(source.at[0], source.at[0])])
-                )
+            meet(turn, 0, 3, 4)
 
             @pl.when(turn == 1)
             def _():
@@ -702,7 +758,8 @@
                 pltpu.VMEM((2, ROWS, HALF), F32),
                 pltpu.VMEM((ROWS, HALF), F32),
                 pltpu.VMEM((4 * ROWS, HALF), F32),
-                pltpu.VMEM((5, 1, 128), F32),
+                pltpu.VMEM((FACES, 1, 128), F32),
+                pltpu.VMEM((1, 128), F32),
                 pltpu.VMEM((6, FACES, QROWS, 128), F32),
                 pltpu.VMEM((6, FACES, QROWS, 128), F32),
                 pltpu.VMEM((6, FACES, QROWS, 128), F32),
@@ -721,6 +778,7 @@
                 pltpu.SemaphoreType.DMA((2, 2)),
                 pltpu.SemaphoreType.DMA((FACES,)),
                 pltpu.SemaphoreType.DMA((FACES,)),
+                pltpu.SemaphoreType.REGULAR((5,)),
             ],
             compiler_params=pltpu.CompilerParams(
                 collective_id=0, has_side_effects=True, vmem_limit_bytes=22 * 1024 * 1024

time: 67.4 us -> 64.7 us (0.960)
  Pallas kernels: 65.1 us -> 62.4 us
    pallas_call x1, Pallas kernels: 65.1 us -> 62.4 us  [shards(): pl.pallas_call(functools.partial(kernel, n_gx, n_gy), out_shape=(jax.Shap...]
where the time goes in v5:
time: 64.7 us; the launch traced here: 64.5 us
  Pallas kernels  62.4 us (96%)
  local copies, waits for them, and re-layouts  1.52 us (2%)
    pallas_call x1, Pallas kernels, shards(): pl.pallas_call(functools.partial(kernel, n_gx, n_gy), out_shape=(jax.Shap...  62.4 us
    pallas_call x2, local copies, waits for them, and re-layouts, shards(): pl.pallas_call(functools.partial(kernel, n_gx, n_gy), out_shape=(jax.Shap...  1.52 us

profile of v5, /device:TPU:1, one launch (start us, length us, event | category | flops | bytes accessed | tf_op | source)
XLA Modules:
  0.0 64.5 jit_solution(14790105802684239634)
XLA Ops:
  0.6 62.4 %shard_map.86 = (f32[2,3,5,5,640]{4,3,2,1,0:T(8,128)S(1)}, f32[2,3,128]{2,1,0:T(4,128)S(1)}) custom-call(s32[1,1,2]{2,1,0:T(1,128)} %bitcast.4, f32[3,2,128]{2,1,0:T(2,128)} %bitcast.3, f32[5,5,640]{2,1,0:T(8,128)} %cond_hbm.1, s32[1,1,128]{2,1,0:T(1,128)} %supp_hbm.1, s32[1,128]{1,0:T(1,128)} %bitcast.5, f32[624,256]{1,0:T(8,128)} %constant.4.clone.mats_hbm, ...), custom_call_target="tpu_custom_call" | custom-call | tf_op jit(solution)/shard_map/pallas_call | solution.py:724
  63.0 0.9 %copy.9 = f32[2,3,5,5,640]{4,0,3,2,1:T(2,128)} copy(f32[2,3,5,5,640]{4,3,2,1,0:T(8,128)S(1)} %get-tuple-element.2) | data formatting | bytes 768000 | tf_op jit(solution)/shard_map/pallas_call | solution.py:724
  63.9 0.6 copy.10

commit v6 on v5

--- a/solution.py
+++ b/solution.py
@@ -164,7 +164,7 @@
 def kernel(
     n_gx, n_gy, tags_hbm, data_hbm, cond_hbm, supp_hbm, nodes_hbm, mats_hbm, cols_hbm, est_ref, res_ref,
     tags_ref, data_ref, cond_ref, supp_ref, nodes_ref, mats_ref, cols_ref, mats, order, spread,
-    fields, second, rates, rhs, prod, ghost_rhs, corner_rhs, sig, gain, gain_out, pick_row, pick_lane, pick_back,
+    fields, second, rates, saved, held, multiple, rhs, prod, ghost_rhs, corner_rhs, sig, gain, gain_out, pick_row, pick_lane, pick_back,
     left, source, ortho, perm, perm_out, beside_support, own_support,
     send_buf, recv_buf, send_next, recv_next, send_diag, recv_diag, red_buf,
     load_sem, send_sem, recv_sem, next_send_sem, next_recv_sem, diag_send_sem, diag_recv_sem, red_send_sem, red_recv_sem,
@@ -286,6 +286,8 @@
         flipped = jnp.transpose(hot).astype(BF16)
         pick_back[0:128, lanes(k)] = flipped
         pick_back[128:256, lanes(k)] = flipped
+    high, low = split(pick_row[...] * pick_row[...])
+    multiple[...] = dot(jnp.concatenate([high, low], axis=1), pick_back[...])
     for comp in range(3):
         for moment in range(2):
             left[0, moment, comp : comp + 1, :] = data_ref[comp, moment : moment + 1, :]
@@ -304,15 +306,12 @@
         gain[:, lanes(k)] = (-DRIVE_GAIN * STEP_SIZE * float(root[k])) * support * cols_ref[:, 0:1]
     own_support[...] = support
 
-    pl.semaphore_wait(barrier, greeted)
     support_copies = [
         remote(
             own_support, beside_support.at[face], supp_send_sem.at[face], supp_recv_sem.at[face], beside[face]
         )
         for face in range(FACES)
     ]
-    for copy, exists in zip(support_copies, to_face):
-        start(copy, exists)
 
     rounds = 0
     while 2**rounds < max(n_gx, n_gy):
@@ -342,7 +341,8 @@
 
     def reduce_send(index, phase, row):
         red_buf[index, phase, 0] = row
-        for step in range(1, sizes[phase]):
+        size = sizes[phase]
+        for step in range(1, size):
             remote(
                 red_buf.at[index, phase, 0], red_buf.at[index, phase, step], red_send_sem.at[index, phase],
                 red_recv_sem.at[index, phase], partner(phase, step),
@@ -461,22 +461,13 @@
         ghost_rhs[face * 16 : face * 16 + 16, lanes(k)] = high
         ghost_rhs[64 + face * 16 : 64 + face * 16 + 16, lanes(k)] = low
 
-    def stage(slot, early, make_second, late, merge, halves_1, halves_2, magnetic_1, magnetic_2, share):
-        load_rhs(fields, magnetic_1)
+    def prepare(slot, magnetic):
+        load_rhs(fields, magnetic)
         out = dot(send_e[...], rhs[:, 0:HALF])
-        if magnetic_1:
+        if magnetic:
             out = out + dot(send_h[...], rhs[:, HALF:WIDE])
-        copies = []
         for face in range(FACES):
             pack_face(out, face, send_buf.at[slot, face])
-            copies.append(
-                remote(
-                    send_buf.at[slot, face], recv_buf.at[slot, face], send_sem.at[slot, face], recv_sem.at[slot, face],
-                    beside[face],
-                )
-            )
-            start(copies[face], to_face[face])
-        corner_copies = []
         for diag in range(4):
             base = 64 + diag * 8
             for tile in range(3):
@@ -484,15 +475,30 @@
                 if tile < 2:
                     piece = jnp.where(sub8 < 4, piece, out[base : base + 8, lanes(2 * tile + 1)])
                 send_diag[slot, diag, 8 * tile : 8 * tile + 8, :] = piece
-            corner_copies.append(
-                remote(
-                    send_diag.at[slot, diag], recv_diag.at[slot, diag], diag_send_sem.at[slot, diag],
-                    diag_recv_sem.at[slot, diag], across[diag],
-                )
+
+    def stage(slot, prepared, first_rates, early, make_second, late, merge, halves_1, halves_2, magnetic_1, magnetic_2, share):
+        if not prepared:
+            prepare(slot, magnetic_1)
+        copies = [
+            remote(
+                send_buf.at[slot, face], recv_buf.at[slot, face], send_sem.at[slot, face], recv_sem.at[slot, face],
+                beside[face],
             )
-            start(corner_copies[diag], to_diag[diag])
+            for face in range(FACES)
+        ]
+        for copy, exists in zip(copies, to_face):
+            start(copy, exists)
+        corner_copies = [
+            remote(
+                send_diag.at[slot, diag], recv_diag.at[slot, diag], diag_send_sem.at[slot, diag],
+                diag_recv_sem.at[slot, diag], across[diag],
+            )
+            for diag in range(4)
+        ]
+        for copy, exists in zip(corner_copies, to_diag):
+            start(copy, exists)
         early()
-        own_rates(fields, rates, halves_1, magnetic_1)
+        own_rates(fields, first_rates, halves_1, magnetic_1)
         make_second()
         load_rhs(second, magnetic_2)
         out = dot(send_e[0:64, :], rhs[:, 0:HALF])
@@ -568,17 +574,15 @@
     def to_output_order(vector, number):
         for moment in range(2):
             both = dot_nt(jnp.concatenate(split(vector[moment]), axis=0), order[...])
-            at = (number * 2 + moment) * ROWS
-            perm_out[at : at + ROWS, :] = both[0:ROWS] + both[ROWS : 2 * ROWS]
+            both = both[0:ROWS] + both[ROWS : 2 * ROWS]
+            for block in range(5):
+                perm_out[number, block, pl.ds(moment, ROWS, stride=2), :] = both[:, lanes(block)]
 
     every, electric = (0, 1), (0,)
 
     def sweep(turn, carry):
-        fields[:, 0:HALF] = inject(turn, 1)
-        fields[:, HALF:WIDE] = jnp.zeros((ROWS, HALF), F32)
-
         def second_1():
-            second[...] = rates[...]
+            pass
 
         def merge_1(lifted):
             second[:, 0:HALF] += lifted[0:ROWS]
@@ -586,18 +590,20 @@
 
         def late_1():
             meet(turn, 0, -1, 0)
+            held[...] = inject(turn, 0)
 
             @pl.when(turn == 1)
             def _():
+                gather(jnp.concatenate(split(saved[...]), axis=0), 1, 1)
                 reduce_send(
                     0, 0, packed_row([data_dot(left[0], left[0]), source_dot(source.at[0], source.at[0])])
                 )
                 to_output_order(source.at[0], 0)
 
-        stage(turn * 3, lambda: meet(turn, 1, 4, 5), second_1, late_1, merge_1, every, every, False, True, 1.0)
+        stage(turn * 3, True, second, lambda: meet(turn, 1, 4, 5), second_1, late_1, merge_1, every, every, False, True, 1.0)
         for k in range(5):
             source[turn, 1, :, lanes(k)] = gain[:, lanes(k)] * (fields[:, lanes(k)] + 0.5 * second[:, lanes(k)])
-        fields[:, 0:HALF] = inject(turn, 0) + fields[:, 0:HALF] + second[:, 0:HALF] + 0.5 * rates[:, 0:HALF]
+        fields[:, 0:HALF] = held[...] + fields[:, 0:HALF] + second[:, 0:HALF] + 0.5 * rates[:, 0:HALF]
         fields[:, HALF:WIDE] = second[:, HALF:WIDE] + 0.5 * rates[:, HALF:WIDE]
 
         def second_2():
@@ -628,12 +634,14 @@
                         column = float(root[k] ** 2) * cols_ref[face * 16 : face * 16 + 16, 5:6]
                         gain_out[face * 16 : face * 16 + 16, lanes(k)] = column * beside_support[face]
 
-        stage(turn * 3 + 1, lambda: meet(turn, 0, 0, 1), second_2, late_2, merge_2, electric, every, True, False, 0.5)
-        fields[:, 0:HALF] = second[:, 0:HALF] + 0.5 * rates[:, 0:HALF]
+        stage(turn * 3 + 1, False, rates, lambda: meet(turn, 0, 0, 1), second_2, late_2, merge_2, electric, every, True, False, 0.5)
+        for k in range(5):
+            first = second[:, lanes(k)] + 0.5 * rates[:, lanes(k)]
+            fields[:, lanes(k)] = first
+            held[:, lanes(k)] = first
         fields[:, HALF:WIDE] = 0.5 * rates[:, HALF:WIDE]
 
         def early_3():
-            gather(rhs[0:160, 0:HALF], turn + 1, 0)
             meet(turn, 0, 2, 3)
 
         def second_3():
@@ -649,6 +657,7 @@
 
         def late_3():
             meet(turn, 0, 3, 4)
+            gather(jnp.concatenate(split(held[...]), axis=0), turn + 1, 0)
 
             @pl.when(turn == 1)
             def _():
@@ -660,30 +669,50 @@
                         ortho[moment, :, lanes(k)] = (
                             source[1, moment, :, lanes(k)] - ratio * source[0, moment, :, lanes(k)]
                         )
+                dots = [
+                    source_dot(ortho, ortho), source_dot(ortho, source.at[0]), data_dot(left[1], left[1]),
+                ]
+                for moment in range(2):
+                    left[0, moment] = left[1, moment] - ratio * left[0, moment]
+                dots += [data_dot(left[0], left[0]), data_dot(left[1], left[0])]
+                red_buf[0, 1, 0] = packed_row(dots)
                 to_output_order(ortho, 1)
 
-        stage(turn * 3 + 2, early_3, second_3, late_3, merge_3, every, electric, True, True, 0.5)
-        halves = split(fields[:, 0:HALF] + rates[:, 0:HALF])
-        gather(jnp.concatenate(halves, axis=0), turn + 1, 1)
+        stage(turn * 3 + 2, False, rates, early_3, second_3, late_3, merge_3, every, electric, True, True, 0.5)
+
+        @pl.when(turn == 0)
+        def _():
+            for k in range(5):
+                last = fields[:, lanes(k)] + rates[:, lanes(k)]
+                saved[:, lanes(k)] = last
+                fields[:, lanes(k)] = multiple[:, lanes(k)] * last
+            fields[:, HALF:WIDE] = jnp.zeros((ROWS, HALF), F32)
+            prepare(3, False)
+
         return carry
 
+    fields[:, 0:HALF] = inject(0, 1)
+    fields[:, HALF:WIDE] = jnp.zeros((ROWS, HALF), F32)
+    prepare(0, False)
+    pl.semaphore_wait(barrier, greeted)
+    for copy, exists in zip(support_copies, to_face):
+        start(copy, exists)
     lax.fori_loop(0, 2, sweep, 0)
+    gather(jnp.concatenate(split(fields[:, 0:HALF] + rates[:, 0:HALF]), axis=0), 2, 1)
 
     norms = red_buf[0, 0, 0]
     sq_b, sq_g = entry(norms, 0), entry(norms, 1)
     ratio = sq_g / sq_b
     for moment in range(2):
-        left[0, moment] = left[1, moment] - ratio * left[0, moment]
         left[2, moment] = left[2, moment] - ratio * left[1, moment]
     p, f, h = left[0], left[1], left[2]
-    products = [
-        data_dot(p, p), source_dot(ortho, ortho), source_dot(ortho, source.at[0]), data_dot(h, h), data_dot(h, f),
-        data_dot(f, f), data_dot(h, p), data_dot(f, p),
-    ]
-    reduce_send(1, 0, packed_row(products))
+    row = red_buf[0, 1, 0]
+    for number, value in ((5, data_dot(h, h)), (6, data_dot(h, f)), (7, data_dot(h, p))):
+        row = jnp.where(lane1 == number, value, row)
+    reduce_send(1, 0, row)
     reduce_send(1, 1, reduce_take(1, 0))
     total = reduce_take(1, 1)
-    pp, oo, og, hh, hf, ff, hp, fp = (entry(total, number) for number in range(8))
+    oo, og, ff, pp, fp, hh, hf, hp = (entry(total, number) for number in range(8))
     take = pp / sq_g
     sq_q = jnp.maximum(oo - 2.0 * take * og + take * take * sq_g, 0.0)
     beta_1 = jnp.sqrt(sq_b)
@@ -705,13 +734,17 @@
     on_h = phi_bar / rho_2 / jnp.sqrt(sq_q)
     on_p = phi_bar / rho_2 * jnp.sqrt(sq_q) / pp
     for moment in range(2):
-        res_ref[moment] = (on_h * (h[moment] - take * f[moment]) - on_p * p[moment])[0:3, :]
+        out = on_h * (h[moment] - take * f[moment]) - on_p * p[moment]
         for comp in range(3):
-            for i in range(5):
-                at = comp * 25 + i * 5
-                one = perm_out[moment * ROWS + at : moment * ROWS + at + 5, :]
-                two = perm_out[(2 + moment) * ROWS + at : (2 + moment) * ROWS + at + 5, :]
-                est_ref[moment, comp, i] = on_first * one + on_ortho * two
+            res_ref[comp, moment : moment + 1, :] = out[comp : comp + 1, :]
+    for tile in range(19):
+        rows = slice(8 * tile, 8 * tile + 8)
+        for block in range(5):
+            value = on_first * perm_out[0, block, rows, :] + on_ortho * perm_out[1, block, rows, :]
+            for part in range(4):
+                node = 4 * tile + part
+                if node < 75:
+                    est_ref[node // 25, node // 5 % 5, node % 5, :, lanes(block)] = value[2 * part : 2 * part + 2, :]
 
 
 def solution(mesh):
@@ -721,11 +754,11 @@
     def shards(probe_data, conductivity, support, face_tags, probe_nodes):
         vmem = pl.BlockSpec(memory_space=pltpu.VMEM)
         anywhere = pl.BlockSpec(memory_space=pl.ANY)
-        return pl.pallas_call(
+        estimate, residual = pl.pallas_call(
             functools.partial(kernel, n_gx, n_gy),
             out_shape=(
-                jax.ShapeDtypeStruct((2, 3, 5, 5, HALF), F32),
-                jax.ShapeDtypeStruct((2, 3, 128), F32),
+                jax.ShapeDtypeStruct((3, 5, 5, 2, HALF), F32),
+                jax.ShapeDtypeStruct((3, 2, 128), F32),
             ),
             in_specs=[anywhere] * 7,
             out_specs=(vmem, vmem),
@@ -743,6 +776,9 @@
                 pltpu.VMEM((ROWS, WIDE), F32),
                 pltpu.VMEM((ROWS, WIDE), F32),
                 pltpu.VMEM((ROWS, WIDE), F32),
+                pltpu.VMEM((ROWS, HALF), F32),
+                pltpu.VMEM((ROWS, HALF), F32),
+                pltpu.VMEM((ROWS, HALF), F32),
                 pltpu.VMEM((256, WIDE), BF16),
                 pltpu.VMEM((INNER, WIDE), F32),
                 pltpu.VMEM((128, HALF), BF16),
@@ -757,7 +793,7 @@
                 pltpu.VMEM((2, 2, ROWS, HALF), F32),
                 pltpu.VMEM((2, ROWS, HALF), F32),
                 pltpu.VMEM((ROWS, HALF), F32),
-                pltpu.VMEM((4 * ROWS, HALF), F32),
+                pltpu.VMEM((2, 5, 2 * ROWS, 128), F32),
                 pltpu.VMEM((FACES, 1, 128), F32),
                 pltpu.VMEM((1, 128), F32),
                 pltpu.VMEM((6, FACES, QROWS, 128), F32),
@@ -792,6 +828,7 @@
                 )
             )
         )
+        return jnp.transpose(estimate, (3, 0, 1, 2, 4)), jnp.transpose(residual, (1, 0, 2))
 
     return jax.shard_map(
         shards,

time: 64.7 us -> 63.6 us (0.983)
  Pallas kernels: 62.4 us -> 61.5 us
    pallas_call x2 -> x0, local copies, waits for them, and re-layouts: 1.52 us -> none  [shards(): pl.pallas_call(functools.partial(kernel, n_gx, n_gy), out_shape=(jax.Shap...]
    unnamed x0 -> x2, local copies, waits for them, and re-layouts: none -> 1.32 us
    pallas_call x1, Pallas kernels: 62.4 us -> 61.5 us  [shards(): pl.pallas_call(functools.partial(kernel, n_gx, n_gy), out_shape=(jax.Shap...]
where the time goes in v6:
time: 63.6 us; the launch traced here: 63.5 us
  Pallas kernels  61.5 us (97%)
  local copies, waits for them, and re-layouts  1.32 us (2%)
  between operations  0.64 us (1%)
    pallas_call x1, Pallas kernels, shards(): pl.pallas_call(functools.partial(kernel, n_gx, n_gy), out_shape=(jax.Shap...  61.5 us
    unnamed x2, local copies, waits for them, and re-layouts  1.32 us

profile of v6, /device:TPU:1, one launch (start us, length us, event | category | flops | bytes accessed | tf_op | source)
XLA Modules:
  0.0 63.5 jit_solution(1900854032709073674)
XLA Ops:
  0.6 61.5 %shard_map.86 = (f32[3,5,5,2,640]{4,3,2,1,0:T(2,128)S(1)}, f32[3,2,128]{2,1,0:T(2,128)S(1)}) custom-call(s32[1,1,2]{2,1,0:T(1,128)} %bitcast.8, f32[3,2,128]{2,1,0:T(2,128)} %bitcast.7, f32[5,5,640]{2,1,0:T(8,128)} %cond_hbm.1, s32[1,1,128]{2,1,0:T(1,128)} %supp_hbm.1, s32[1,128]{1,0:T(1,128)} %bitcast.9, f32[624,256]{1,0:T(8,128)} %constant.4.clone.mats_hbm, ...), custom_call_target="tpu_custom_call" | custom-call | tf_op jit(solution)/shard_map/pallas_call | solution.py:757
  62.2 0.7 %copy.11 = f32[2,3,5,5,640]{4,0,3,2,1:T(2,128)} copy(f32[2,3,5,5,640]{4,0,3,2,1:T(2,128)S(1)} %bitcast.5) | data formatting | bytes 768000
  62.9 0.6 copy.12

commit v7 on v6

--- a/solution.py
+++ b/solution.py
@@ -381,14 +381,13 @@
                 total = total + a[moment, :, lanes(k)] * b[moment, :, lanes(k)]
         return whole(total)
 
-    def load_rhs(ref, magnetic):
-        for block in range(10 if magnetic else 5):
-            high, low = split(ref[:, lanes(block)])
-            rhs[0:80, lanes(block)] = high
-            rhs[80:160, lanes(block)] = low
-            rhs[160:240, lanes(block)] = high
-
-    def own_rates(field, result, halves, magnetic):
+    def put_rhs(block, value):
+        high, low = split(value)
+        rhs[0:80, lanes(block)] = high
+        rhs[80:160, lanes(block)] = low
+        rhs[160:240, lanes(block)] = high
+
+    def own_rates(field, halves, magnetic, emit):
         if not magnetic:
             prod[:, 0:HALF] = dot(inner[...], rhs[:, 0:HALF])
         elif len(halves) == 1:
@@ -410,8 +409,7 @@
                         inward = pltpu.roll(field[0:QROWS, lanes(0)], 127, 1)
                         edge = -tag_high * field[0:QROWS, lanes(4)]
                         upper = upper + spread[2][0:QROWS] * jnp.where(lane56 == 127, edge, inward)
-                    result[0:QROWS, lanes(k)] = upper
-                    result[QROWS:ROWS, lanes(k)] = change[QROWS:ROWS]
+                    emit(k, jnp.concatenate([upper, change[QROWS:ROWS]], axis=0))
                     continue
                 slope = None
                 for m in range(5):
@@ -435,8 +433,7 @@
                         edge = (tag_high * -sign) * (own_high + turn_high)
                         incoming = jnp.where(lane56 == 127, edge, inward)
                     upper = upper + spread[2][0:QROWS] * incoming
-                result[0:QROWS, lanes(own0 + k)] = upper
-                result[QROWS:ROWS, lanes(own0 + k)] = change[QROWS:ROWS]
+                emit(own0 + k, jnp.concatenate([upper, change[QROWS:ROWS]], axis=0))
 
     def pack_face(out, face, buf):
         base = face * 16
@@ -462,7 +459,6 @@
         ghost_rhs[64 + face * 16 : 64 + face * 16 + 16, lanes(k)] = low
 
     def prepare(slot, magnetic):
-        load_rhs(fields, magnetic)
         out = dot(send_e[...], rhs[:, 0:HALF])
         if magnetic:
             out = out + dot(send_h[...], rhs[:, HALF:WIDE])
@@ -476,9 +472,7 @@
                     piece = jnp.where(sub8 < 4, piece, out[base : base + 8, lanes(2 * tile + 1)])
                 send_diag[slot, diag, 8 * tile : 8 * tile + 8, :] = piece
 
-    def stage(slot, prepared, first_rates, early, make_second, late, merge, halves_1, halves_2, magnetic_1, magnetic_2, share):
-        if not prepared:
-            prepare(slot, magnetic_1)
+    def stage(slot, early, first_block, late, merge, finish, halves_1, halves_2, magnetic_1, magnetic_2, share):
         copies = [
             remote(
                 send_buf.at[slot, face], recv_buf.at[slot, face], send_sem.at[slot, face], recv_sem.at[slot, face],
@@ -498,9 +492,7 @@
         for copy, exists in zip(corner_copies, to_diag):
             start(copy, exists)
         early()
-        own_rates(fields, first_rates, halves_1, magnetic_1)
-        make_second()
-        load_rhs(second, magnetic_2)
+        own_rates(fields, halves_1, magnetic_1, first_block)
         out = dot(send_e[0:64, :], rhs[:, 0:HALF])
         if magnetic_2:
             out = out + dot(send_h[0:64, :], rhs[:, HALF:WIDE])
@@ -521,8 +513,11 @@
             for k in range(5):
                 set_ghosts(face, k, unpack_face(recv_buf.at[slot, face], k))
         merge(dot(lift[...], ghost_rhs[...]))
-        load_rhs(second, magnetic_2)
-        own_rates(second, rates, halves_2, magnetic_2)
+
+        def store(block, value):
+            rates[:, lanes(block)] = value
+
+        own_rates(second, halves_2, magnetic_2, store)
 
         wait_all(corner_copies, to_diag, 3)
         for two in range(2):
@@ -546,12 +541,7 @@
                     piece = piece + strength * unpack_face(send_buf.at[slot, face ^ 1], k)
                     piece = piece * gain_out[face * 16 : face * 16 + 16, lanes(k)]
                 set_ghosts(face, k, unpack_face(recv_next.at[slot, face], k) + share * piece)
-        if len(halves_2) == 2:
-            lifted = dot(lift[...], ghost_rhs[...])
-            rates[:, 0:HALF] += lifted[0:ROWS]
-            rates[:, HALF:WIDE] += lifted[ROWS : 2 * ROWS]
-        else:
-            rates[:, 0:HALF] += dot(lift[0:ROWS, :], ghost_rhs[...])
+        finish(dot(lift[...] if len(halves_2) == 2 else lift[0:ROWS, :], ghost_rhs[...]))
 
     def inject(turn, moment):
         values = jnp.where(
@@ -581,12 +571,31 @@
     every, electric = (0, 1), (0,)
 
     def sweep(turn, carry):
-        def second_1():
-            pass
+        def set_second(block, value):
+            second[:, lanes(block)] = value
+            put_rhs(block, value)
+
+        def set_fields(block, value):
+            fields[:, lanes(block)] = value
+            put_rhs(block, value)
+
+        def lifted_block(lifted, block):
+            return lifted[block // 5 * ROWS : (block // 5 + 1) * ROWS, lanes(block % 5)]
 
         def merge_1(lifted):
-            second[:, 0:HALF] += lifted[0:ROWS]
-            second[:, HALF:WIDE] += lifted[ROWS : 2 * ROWS]
+            for block in range(10):
+                set_second(block, second[:, lanes(block)] + lifted_block(lifted, block))
+
+        def finish_1(lifted):
+            for block in range(10):
+                slope = second[:, lanes(block)]
+                value = slope + 0.5 * (rates[:, lanes(block)] + lifted_block(lifted, block))
+                if block < 5:
+                    start = fields[:, lanes(block)]
+                    source[turn, 1, :, lanes(block)] = gain[:, lanes(block)] * (start + 0.5 * slope)
+                    value = value + start + held[:, lanes(block)]
+                set_fields(block, value)
+            prepare(turn * 3 + 1, True)
 
         def late_1():
             meet(turn, 0, -1, 0)
@@ -600,27 +609,33 @@
                 )
                 to_output_order(source.at[0], 0)
 
-        stage(turn * 3, True, second, lambda: meet(turn, 1, 4, 5), second_1, late_1, merge_1, every, every, False, True, 1.0)
-        for k in range(5):
-            source[turn, 1, :, lanes(k)] = gain[:, lanes(k)] * (fields[:, lanes(k)] + 0.5 * second[:, lanes(k)])
-        fields[:, 0:HALF] = held[...] + fields[:, 0:HALF] + second[:, 0:HALF] + 0.5 * rates[:, 0:HALF]
-        fields[:, HALF:WIDE] = second[:, HALF:WIDE] + 0.5 * rates[:, HALF:WIDE]
-
-        def second_2():
-            for k in range(5):
-                amount = gain[:, lanes(k)] * (fields[:, lanes(k)] + 0.5 * rates[:, lanes(k)])
-                source[turn, 0, :, lanes(k)] = amount
-                second[:, lanes(k)] = gain[:, lanes(k)] * amount
-            second[:, HALF:WIDE] = jnp.zeros((ROWS, HALF), F32)
+        stage(
+            turn * 3, lambda: meet(turn, 1, 4, 5), set_second, late_1, merge_1, finish_1, every, every, False, True, 1.0
+        )
+
+        def block_2(k, value):
+            amount = gain[:, lanes(k)] * (fields[:, lanes(k)] + 0.5 * value)
+            source[turn, 0, :, lanes(k)] = amount
+            set_second(k, gain[:, lanes(k)] * amount)
 
         def merge_2(lifted):
             for k in range(5):
                 amount = source[turn, 0, :, lanes(k)] + 0.5 * gain[:, lanes(k)] * lifted[0:ROWS, lanes(k)]
                 source[turn, 0, :, lanes(k)] = amount
-                second[:, lanes(k)] = gain[:, lanes(k)] * amount
+                set_second(k, gain[:, lanes(k)] * amount)
+
+        def finish_2(lifted):
+            for block in range(10):
+                value = 0.5 * (rates[:, lanes(block)] + lifted_block(lifted, block))
+                if block < 5:
+                    value = value + second[:, lanes(block)]
+                    held[:, lanes(block)] = value
+                set_fields(block, value)
+            prepare(turn * 3 + 2, True)
 
         def late_2():
             meet(turn, 0, 1, 2)
+            second[:, HALF:WIDE] = jnp.zeros((ROWS, HALF), F32)
 
             @pl.when(turn == 1)
             def _():
@@ -634,29 +649,30 @@
                         column = float(root[k] ** 2) * cols_ref[face * 16 : face * 16 + 16, 5:6]
                         gain_out[face * 16 : face * 16 + 16, lanes(k)] = column * beside_support[face]
 
-        stage(turn * 3 + 1, False, rates, lambda: meet(turn, 0, 0, 1), second_2, late_2, merge_2, electric, every, True, False, 0.5)
-        for k in range(5):
-            first = second[:, lanes(k)] + 0.5 * rates[:, lanes(k)]
-            fields[:, lanes(k)] = first
-            held[:, lanes(k)] = first
-        fields[:, HALF:WIDE] = 0.5 * rates[:, HALF:WIDE]
+        stage(
+            turn * 3 + 1, lambda: meet(turn, 0, 0, 1), block_2, late_2, merge_2, finish_2, electric, every, True, False, 0.5
+        )
 
         def early_3():
             meet(turn, 0, 2, 3)
 
-        def second_3():
-            for k in range(5):
-                drive = gain[:, lanes(k)] * source[turn, 1, :, lanes(k)]
-                second[:, lanes(k)] = fields[:, lanes(k)] + 0.5 * (rates[:, lanes(k)] + drive)
-                fields[:, lanes(k)] = fields[:, lanes(k)] + drive
-            second[:, HALF:WIDE] = fields[:, HALF:WIDE] + 0.5 * rates[:, HALF:WIDE]
+        def block_3(block, value):
+            if block < 5:
+                value = value + gain[:, lanes(block)] * source[turn, 1, :, lanes(block)]
+            set_second(block, fields[:, lanes(block)] + 0.5 * value)
 
         def merge_3(lifted):
-            second[:, 0:HALF] += 0.5 * lifted[0:ROWS]
-            second[:, HALF:WIDE] += 0.5 * lifted[ROWS : 2 * ROWS]
+            for block in range(10):
+                set_second(block, second[:, lanes(block)] + 0.5 * lifted_block(lifted, block))
+
+        def finish_3(lifted):
+            for k in range(5):
+                saved[:, lanes(k)] = fields[:, lanes(k)] + rates[:, lanes(k)] + lifted[:, lanes(k)]
 
         def late_3():
             meet(turn, 0, 3, 4)
+            for k in range(5):
+                fields[:, lanes(k)] = fields[:, lanes(k)] + gain[:, lanes(k)] * source[turn, 1, :, lanes(k)]
             gather(jnp.concatenate(split(held[...]), axis=0), turn + 1, 0)
 
             @pl.when(turn == 1)
@@ -678,27 +694,28 @@
                 red_buf[0, 1, 0] = packed_row(dots)
                 to_output_order(ortho, 1)
 
-        stage(turn * 3 + 2, False, rates, early_3, second_3, late_3, merge_3, every, electric, True, True, 0.5)
+        stage(turn * 3 + 2, early_3, block_3, late_3, merge_3, finish_3, every, electric, True, True, 0.5)
 
         @pl.when(turn == 0)
         def _():
             for k in range(5):
-                last = fields[:, lanes(k)] + rates[:, lanes(k)]
-                saved[:, lanes(k)] = last
-                fields[:, lanes(k)] = multiple[:, lanes(k)] * last
+                set_fields(k, multiple[:, lanes(k)] * saved[:, lanes(k)])
             fields[:, HALF:WIDE] = jnp.zeros((ROWS, HALF), F32)
             prepare(3, False)
 
         return carry
 
-    fields[:, 0:HALF] = inject(0, 1)
+    first_input = inject(0, 1)
+    fields[:, 0:HALF] = first_input
+    for k in range(5):
+        put_rhs(k, first_input[:, lanes(k)])
     fields[:, HALF:WIDE] = jnp.zeros((ROWS, HALF), F32)
     prepare(0, False)
     pl.semaphore_wait(barrier, greeted)
     for copy, exists in zip(support_copies, to_face):
         start(copy, exists)
     lax.fori_loop(0, 2, sweep, 0)
-    gather(jnp.concatenate(split(fields[:, 0:HALF] + rates[:, 0:HALF]), axis=0), 2, 1)
+    gather(jnp.concatenate(split(saved[...]), axis=0), 2, 1)
 
     norms = red_buf[0, 0, 0]
     sq_b, sq_g = entry(norms, 0), entry(norms, 1)

time: 63.6 us -> 63.6 us (level)
  no operation moved by 1% of the time
where the time goes in v7:
time: 63.6 us; the launch traced here: 63.4 us
  Pallas kernels  61.5 us (97%)
  local copies, waits for them, and re-layouts  1.32 us (2%)
  between operations  0.64 us (1%)
    pallas_call x1, Pallas kernels, shards(): pl.pallas_call(functools.partial(kernel, n_gx, n_gy), out_shape=(jax.Shap...  61.5 us
    unnamed x2, local copies, waits for them, and re-layouts  1.32 us

profile of v7, /device:TPU:1, one launch (start us, length us, event | category | flops | bytes accessed | tf_op | source)
XLA Modules:
  0.0 63.4 jit_solution(11064136256165554653)
XLA Ops:
  0.6 61.5 %shard_map.86 = (f32[3,5,5,2,640]{4,3,2,1,0:T(2,128)S(1)}, f32[3,2,128]{2,1,0:T(2,128)S(1)}) custom-call(s32[1,1,2]{2,1,0:T(1,128)} %bitcast.8, f32[3,2,128]{2,1,0:T(2,128)} %bitcast.7, f32[5,5,640]{2,1,0:T(8,128)} %cond_hbm.1, s32[1,1,128]{2,1,0:T(1,128)} %supp_hbm.1, s32[1,128]{1,0:T(1,128)} %bitcast.9, f32[624,256]{1,0:T(8,128)} %constant.4.clone.mats_hbm, ...), custom_call_target="tpu_custom_call" | custom-call | tf_op jit(solution)/shard_map/pallas_call | solution.py:774
  62.1 0.7 %copy.11 = f32[2,3,5,5,640]{4,0,3,2,1:T(2,128)} copy(f32[2,3,5,5,640]{4,0,3,2,1:T(2,128)S(1)} %bitcast.5) | data formatting | bytes 768000
  62.8 0.6 copy.12
